TPU v7x, 512 devices: a whole 4x4x16 slice. The times are simulated.
512 devices in a mesh: dp: 32 (over y, z_hi, core), hidden: 16 (over x, z_lo).
Axes of the slice: x: 4, y: 4, z: 16 (z_hi: 4, z_lo: 4; z = z_hi * 4 + z_lo), core: 2. Of those that a mesh axis runs over, the one named last changes fastest.
Arguments:
- grad_out: bfloat16 [4096, 8192], P('dp', 'hidden'), may hold values from -6 to 6
- signs: int32 [8192], P('hidden'), may hold values from 0 to 1
- weight: bfloat16 [16384, 8192], P('dp', 'hidden'), may hold values from -0.046875 to 0.046875
- activations: bfloat16 [4096, 16384], P('hidden', 'dp'), may hold values from -15 to 15
- outliers: int32 [128], replicated, may hold values from 0 to 16383
Outputs:
- input_grad: bfloat16 [4096, 16384], P('hidden', 'dp')
- weight_grad: float32 [16384, 8192], P('dp', 'hidden')
Inputs may be any that keep to these rules, and one draw needn't show every extreme that they name: `outliers`: entries may repeat.
All inputs are finite; a program needn't handle non-finite values.
Results may differ from a plain program's by a relative error of at most 0.023.
Values may be sent and summed in bfloat16 or wider, within the bound.
No kernel may reach another device: no remote copies, remote signals or barrier semaphores. Data moves between devices by JAX's collectives and lax.ppermute only.
A program may use at most 64 MiB of HBM per device.

v0:
```python
import math

import jax
import jax.numpy as jnp
from jax import lax
from jax.sharding import PartitionSpec as P


def swapped(array, axis, apart):
    return lax.ppermute(array, axis, [(i, i ^ 1 << apart) for i in range(lax.axis_size(axis))])


def hadamard_table(order):
    index = jnp.arange(order, dtype=jnp.int32)
    count = jnp.zeros((order, order), jnp.int32)
    for level in range(order.bit_length() - 1):
        step = 2**level
        count = count + index[:, None] // step % 2 * (index[None, :] // step % 2)
    return jnp.where(count % 2 == 0, 1.0, -1.0).astype(jnp.float32)


def on_device(grad_out, signs, weight, activations, outliers):
    tok_rows, width = grad_out.shape
    groups = lax.axis_size("hidden")
    total = width * groups
    factor = 1.0 / math.sqrt(total)
    token_scale = 1.0 / math.sqrt(tok_rows * lax.axis_size("dp"))
    flips = (2 * signs - 1).astype(jnp.bfloat16)
    signed = grad_out * flips[None, :]
    local = jnp.dot(
        signed, hadamard_table(width).astype(jnp.bfloat16), preferred_element_type=jnp.float32
    )
    for level in range(groups.bit_length() - 1):
        partner = swapped(local, "hidden", level)
        upper = lax.axis_index("hidden") // 2**level % 2 == 1
        local = jnp.where(upper, partner - local, local + partner)
    rotated = (local * factor).astype(jnp.bfloat16)
    act_rows, ff_local = activations.shape
    channel = lax.axis_index("dp") * ff_local + jnp.arange(ff_local, dtype=jnp.int32)
    special = jnp.any(channel[:, None] == outliers[None, :], axis=1)
    clipped = jnp.where(special[None, :], activations, jnp.clip(activations, -3.0, 3.0))
    kept = special[None, :] | (jnp.abs(activations.astype(jnp.float32)) <= 3.0)
    gathered = lax.all_gather(rotated, "dp", axis=0, tiled=True)
    rows_part = gathered
    summed = lax.psum_scatter(
        jnp.dot(rows_part, weight.T, preferred_element_type=jnp.float32).astype(jnp.bfloat16),
        "hidden",
        scatter_dimension=0,
        tiled=True,
    ).astype(jnp.float32)
    rows_part = gathered
    weight_sum = jnp.dot(
        lax.all_gather(clipped, "hidden", axis=0, tiled=True).T,
        rows_part,
        preferred_element_type=jnp.float32,
    )
    weight_grad = weight_sum * token_scale
    input_grad = jnp.where(kept, summed, 0.0).astype(jnp.bfloat16)
    return (input_grad, weight_grad)


def solution(mesh):
    in_specs = (P("dp", "hidden"), P("hidden"), P("dp", "hidden"), P("hidden", "dp"), P())
    out_specs = (P("hidden", "dp"), P("dp", "hidden"))
    return jax.shard_map(
        on_device, mesh=mesh, in_specs=in_specs, out_specs=out_specs, check_vma=False
    )
```

profile of v0, /device:TPU:1, one launch (start us, length us, event | category | flops | bytes accessed | tf_op | source)
XLA Modules:
  0.0 375.7 jit_solution(12794763083362499513)
XLA Ops:
  7.2 0.0 copy-start
  7.2 0.0 all-gather.3.cloned.1.call-start
  7.3 0.7 add_select_fusion.20
  8.0 0.0 copy-start.2
  8.0 0.0 copy-start.1
  8.0 2.2 fusion.2
  10.3 4.4 %collective-permute-start = (f32[128,512]{1,0:T(8,128)S(1)}, f32[128,512]{1,0:T(8,128)S(1)}, u32[]{:S(2)}, u32[]{:S(2)}) collective-permute-start(f32[128,512]{1,0:T(8,128)S(1)} %fusion.2), channel_id=1, source_target_pairs={{0,1},{1,0},{2,3},{3,2},{4,5},{5,4},{6,7},{7,6},{8,9},{9,8},{10,11... | collective-permute-start | bytes 786440 | tf_op jit(solution)/shard_map/ppermute | solution.py:10
  14.7 3.7 collective-permute-done
  18.4 7.1 %collective-permute-start.1 = (f32[128,512]{1,0:T(8,128)S(1)}, f32[128,512]{1,0:T(8,128)S(1)}, u32[]{:S(2)}, u32[]{:S(2)}) collective-permute-start(f32[128,512]{1,0:T(8,128)S(1)} %add_select_fusion.3), channel_id=1, source_target_pairs={{0,2},{1,3},{2,0},{3,1},{4,6},{5,7},{6,4},{7,5},{8,10},{9,11},{10,... | collective-permute-start | bytes 786440 | tf_op jit(solution)/shard_map/ppermute | solution.py:10
  25.5 11.1 %collective-permute-done.1 = f32[128,512]{1,0:T(8,128)S(1)} collective-permute-done((f32[128,512]{1,0:T(8,128)S(1)}, f32[128,512]{1,0:T(8,128)S(1)}, u32[]{:S(2)}, u32[]{:S(2)}) %collective-permute-start.1) | collective-permute-done | bytes 262176 | tf_op jit(solution)/shard_map/ppermute | solution.py:10
  36.6 3.3 collective-permute-start.2
  40.0 4.5 %collective-permute-done.2 = f32[128,512]{1,0:T(8,128)S(1)} collective-permute-done((f32[128,512]{1,0:T(8,128)S(1)}, f32[128,512]{1,0:T(8,128)S(1)}, u32[]{:S(2)}, u32[]{:S(2)}) %collective-permute-start.2) | collective-permute-done | bytes 262176 | tf_op jit(solution)/shard_map/ppermute | solution.py:10
  44.6 5.2 %collective-permute-start.3 = (f32[128,512]{1,0:T(8,128)S(1)}, f32[128,512]{1,0:T(8,128)S(1)}, u32[]{:S(2)}, u32[]{:S(2)}) collective-permute-start(f32[128,512]{1,0:T(8,128)S(1)} %add_select_fusion.1), channel_id=1, source_target_pairs={{0,8},{1,9},{2,10},{3,11},{4,12},{5,13},{6,14},{7,15},{8,0},{9,1},... | collective-permute-start | bytes 786440 | tf_op jit(solution)/shard_map/ppermute | solution.py:10
  49.8 3.7 collective-permute-done.3
  53.5 0.7 multiply_convert_fusion
  54.2 0.0 all-gather.3.cloned.1.call-update
  54.2 0.0 all-gather.5.cloned.1.call-start
  54.3 0.0 copy-done.2
  54.3 0.2 compare_reduce_fusion
  54.6 0.0 copy-done.1
  54.6 0.7 clamp_select_fusion
  55.3 0.0 all-gather.5.cloned.1.call-update
  55.3 0.0 reduce-scatter.2.cloned.1.call-start
  55.4 103.1 %all-gather.3.cloned.1.call-done = bf16[4096,512]{1,0:T(8,128)(2,1)} async-done(((bf16[128,512]{1,0:T(8,128)(2,1)}), bf16[4096,512]{1,0:T(8,128)(2,1)}) %all-gather.3.cloned.1.call-update) | async-done | bytes 4194320 | tf_op jit(solution)/shard_map/all_gather | solution.py:43
  158.4 0.0 copy-done
  158.4 6.5 %convolution_convert_fusion = bf16[4096,512]{1,0:T(8,128)(2,1)} fusion(bf16[4096,512]{1,0:T(8,128)(2,1)} %all-gather.3.cloned.1.call-done, bf16[512,512]{1,0:T(8,128)(2,1)S(1)} %copy-done), kind=kOutput, calls=%fused_computation | convolution fusion | flops 2149580800 | bytes 8912896 | tf_op jit(solution)/shard_map/dot_general | solution.py:46
  165.0 0.0 reduce-scatter.2.cloned.1.call-update
  165.0 97.2 %all-gather.5.cloned.1.call-done = bf16[4096,512]{1,0:T(8,128)(2,1)} async-done(((bf16[256,512]{1,0:T(8,128)(2,1)}), bf16[4096,512]{1,0:T(8,128)(2,1)}) %all-gather.5.cloned.1.call-update) | async-done | bytes 4194320 | tf_op jit(solution)/shard_map/all_gather | solution.py:53
  262.2 6.8 %convolution_multiply_fusion = f32[512,512]{1,0:T(8,128)} fusion(bf16[4096,512]{1,0:T(8,128)(2,1)} %all-gather.5.cloned.1.call-done, bf16[4096,512]{1,0:T(8,128)(2,1)} %all-gather.3.cloned.1.call-done), kind=kOutput, calls=%fused_computation.4 | convolution fusion | flops 2147745792 | bytes 9437184 | tf_op jit(solution)/shard_map/dot_general | solution.py:52
  269.0 98.3 %reduce-scatter.2.cloned.1.call-done = bf16[256,512]{1,0:T(8,128)(2,1)} async-done(((bf16[4096,512]{1,0:T(8,128)(2,1)}), bf16[256,512]{1,0:T(8,128)(2,1)}) %reduce-scatter.2.cloned.1.call-update) | async-done | bytes 262160 | tf_op jit(solution)/shard_map/reduce_scatter | solution.py:45
  367.3 1.8 select_convert_fusion.2
  (8 shorter events, 0.1 us)
Async XLA Ops:
  7.2 151.3 %copy-start = (bf16[512,512]{1,0:T(8,128)(2,1)S(1)}, bf16[512,512]{1,0:T(8,128)(2,1)}, u32[]{:S(2)}) copy-start(bf16[512,512]{1,0:T(8,128)(2,1)} %param.7) | copy-start | bytes 1572868
  7.2 151.3 %all-gather.3.cloned.1.call-start = ((), (), s32[]{:S(2)}) async-start(), calls=%async_computation.1 | async-start | bytes 4325376 | tf_op jit(solution)/shard_map/all_gather | solution.py:43
  8.0 46.3 %copy-start.2 = (s32[128]{0:T(128)S(1)}, s32[128]{0:T(128)}, u32[]{:S(2)}) copy-start(s32[128]{0:T(128)} %param.9) | copy-start | bytes 1540
  8.0 46.5 %copy-start.1 = (bf16[256,512]{1,0:T(8,128)(2,1)S(1)}, bf16[256,512]{1,0:T(8,128)(2,1)}, u32[]{:S(2)}) copy-start(bf16[256,512]{1,0:T(8,128)(2,1)} %param.8) | copy-start | bytes 786436
  10.3 8.1 %collective-permute-start = (f32[128,512]{1,0:T(8,128)S(1)}, f32[128,512]{1,0:T(8,128)S(1)}, u32[]{:S(2)}, u32[]{:S(2)}) collective-permute-start(f32[128,512]{1,0:T(8,128)S(1)} %fusion.2), channel_id=1, source_target_pairs={{0,1},{1,0},{2,3},{3,2},{4,5},{5,4},{6,7},{7,6},{8,9},{9,8},{10,11... | collective-permute-start | bytes 786440 | tf_op jit(solution)/shard_map/ppermute | solution.py:10
  18.4 18.2 %collective-permute-start.1 = (f32[128,512]{1,0:T(8,128)S(1)}, f32[128,512]{1,0:T(8,128)S(1)}, u32[]{:S(2)}, u32[]{:S(2)}) collective-permute-start(f32[128,512]{1,0:T(8,128)S(1)} %add_select_fusion.3), channel_id=1, source_target_pairs={{0,2},{1,3},{2,0},{3,1},{4,6},{5,7},{6,4},{7,5},{8,10},{9,11},{10,... | collective-permute-start | bytes 786440 | tf_op jit(solution)/shard_map/ppermute | solution.py:10
  36.6 7.9 %collective-permute-start.2 = (f32[128,512]{1,0:T(8,128)S(1)}, f32[128,512]{1,0:T(8,128)S(1)}, u32[]{:S(2)}, u32[]{:S(2)}) collective-permute-start(f32[128,512]{1,0:T(8,128)S(1)} %add_select_fusion.2), channel_id=1, source_target_pairs={{0,4},{1,5},{2,6},{3,7},{4,0},{5,1},{6,2},{7,3},{8,12},{9,13},{10,... | collective-permute-start | bytes 786440 | tf_op jit(solution)/shard_map/ppermute | solution.py:10
  44.6 8.9 %collective-permute-start.3 = (f32[128,512]{1,0:T(8,128)S(1)}, f32[128,512]{1,0:T(8,128)S(1)}, u32[]{:S(2)}, u32[]{:S(2)}) collective-permute-start(f32[128,512]{1,0:T(8,128)S(1)} %add_select_fusion.1), channel_id=1, source_target_pairs={{0,8},{1,9},{2,10},{3,11},{4,12},{5,13},{6,14},{7,15},{8,0},{9,1},... | collective-permute-start | bytes 786440 | tf_op jit(solution)/shard_map/ppermute | solution.py:10
  54.2 208.0 %all-gather.5.cloned.1.call-start = ((), (), s32[]{:S(2)}) async-start(), calls=%async_computation.3 | async-start | bytes 4456448 | tf_op jit(solution)/shard_map/all_gather | solution.py:53
  55.3 312.0 %reduce-scatter.2.cloned.1.call-start = ((), (), s32[]{:S(2)}) async-start(), calls=%async_computation.2 | async-start | bytes 4456448 | tf_op jit(solution)/shard_map/reduce_scatter | solution.py:45
Sparse Core Ops, SparseCore 0:
  54.4 104.0 all-gather.2
  161.1 101.1 all-gather.4
  265.1 102.2 reduce-scatter.1
where the time goes:
time: 379 us; the launch traced here: 376 us
  waiting for transfers between devices  322 us (85%)
  starting transfers between devices  20.1 us (5%)
  matrix products  15.6 us (4%)
  between operations  14 us (4%)
  other arithmetic  4.35 us (1%)
    all_gather x1, waiting for transfers between devices, on_device(): gathered = lax.all_gather(rotated, 'dp', axis=0, tiled=True)  103 us
    reduce_scatter x1, waiting for transfers between devices, on_device(): lax.psum_scatter(jnp.dot(rows_part, weight.T, preferred_element_type=jnp....  98.3 us
    all_gather x1, waiting for transfers between devices, on_device(): lax.all_gather(clipped, 'hidden', axis=0, tiled=True)  97.2 us
    ppermute x4, waiting for transfers between devices, swapped(): lax.ppermute(array, axis, [(i, i ^ 1 << apart) for i in range(lax.axis_si...  23 us
    ppermute x4, starting transfers between devices, swapped(): lax.ppermute(array, axis, [(i, i ^ 1 << apart) for i in range(lax.axis_si...  19.9 us
  transfers between devices with their start and end apart: 7, of which 7 were waited for; matrix products, arithmetic and copies ran while one was open for 4% of the time, Pallas kernels for 0%

commit v1 on v0

v1 whole, which is shorter than its diff:
```python
import math

import jax
import jax.numpy as jnp
from jax import lax
from jax.sharding import Mesh, PartitionSpec as P


def hadamard_table(order):
    index = jnp.arange(order, dtype=jnp.int32)
    count = jnp.zeros((order, order), jnp.int32)
    for level in range(order.bit_length() - 1):
        step = 2**level
        count = count + index[:, None] // step % 2 * (index[None, :] // step % 2)
    return jnp.where(count % 2 == 0, 1.0, -1.0).astype(jnp.float32)


def rotate_rows(rows, width):
    groups = rows.shape[0] // 8
    local = jnp.dot(
        rows, hadamard_table(width).astype(jnp.bfloat16), preferred_element_type=jnp.float32
    )
    local = local.reshape(groups, 8, width)
    step = 1
    while step < groups:
        pairs = local.reshape(groups // (2 * step), 2, step, 8, width)
        low, high = pairs[:, 0], pairs[:, 1]
        local = jnp.stack([low + high, low - high], axis=1).reshape(groups, 8, width)
        step *= 2
    return local


def on_device(grad_out, signs, weight, activations, outliers):
    n_y, n_zh, n_x, n_zl = (lax.axis_size(a) for a in ("y", "zh", "x", "zl"))
    hidden = n_x * n_zl
    tok, width = grad_out.shape
    act_rows, ff = activations.shape
    per = tok // hidden
    quarter = tok // n_x
    total = width * hidden
    factor = 1.0 / math.sqrt(total)
    token_scale = 1.0 / math.sqrt(tok * n_y * n_zh * 2)
    core = lax.axis_index("c")

    weights = lax.all_gather(weight, "x", axis=1, tiled=True)

    flips = (2 * signs - 1).astype(jnp.bfloat16)
    signed = grad_out * flips[None, :]
    rows = lax.all_to_all(signed, ("x", "zl"), split_axis=0, concat_axis=0, tiled=True)
    rotated = (rotate_rows(rows, width) * factor).astype(jnp.bfloat16)
    pieces = rotated.reshape(n_x, n_zl, per, width).transpose(1, 2, 0, 3)
    pieces = pieces.reshape(n_zl, per, n_x * width)
    spread = jnp.broadcast_to(pieces[None], (n_zh, n_zl, per, n_x * width))
    spread = spread.reshape(n_zh * n_zl * per, n_x * width)
    mine = lax.all_to_all(spread, ("zh", "zl"), split_axis=0, concat_axis=0, tiled=True)
    own = lax.all_gather(mine, "y", axis=0, tiled=True)
    other = lax.ppermute(own, "c", [(0, 1), (1, 0)])

    channel = (
        (lax.axis_index("y") * n_zh + lax.axis_index("zh")) * 2 + core
    ) * ff + jnp.arange(ff, dtype=jnp.int32)
    special = jnp.any(channel[:, None] == outliers[None, :], axis=1)
    clipped = jnp.where(special[None, :], activations, jnp.clip(activations, -3.0, 3.0))
    clipped = clipped.reshape(2, n_x, quarter, ff).transpose(1, 0, 2, 3)
    clipped = clipped.reshape(n_x * 2 * quarter, ff)
    swapped = lax.all_to_all(clipped, "x", split_axis=0, concat_axis=0, tiled=True)
    acts = lax.all_gather(swapped, "zl", axis=0, tiled=True)
    acts = acts.reshape(n_zl, n_x, 2, quarter, ff).transpose(2, 1, 0, 3, 4)
    acts = acts.reshape(2, hidden * quarter, ff)
    acts_own = jnp.where(core == 0, acts[0], acts[1])
    acts_other = jnp.where(core == 0, acts[1], acts[0])

    def product(a, b, dims):
        return lax.dot_general(a, b, (dims, ((), ())), preferred_element_type=jnp.float32)

    wg = product(acts_own, own, ((0,), (0,))) + product(acts_other, other, ((0,), (0,)))
    wg = (wg * token_scale).astype(jnp.bfloat16).reshape(ff, n_x, width).transpose(1, 0, 2)
    wg = lax.psum_scatter(wg, "x", scatter_dimension=0, tiled=True)
    weight_grad = wg.reshape(ff, width).astype(jnp.float32)

    parts = [
        product(half, weights, ((1,), (1,))).astype(jnp.bfloat16).reshape(hidden, 1, quarter, ff)
        for half in (own, other)
    ]
    parts = jnp.concatenate(parts, axis=1).reshape(hidden * 2 * quarter, ff)
    parts = lax.all_to_all(parts, ("x", "zl"), split_axis=0, concat_axis=0, tiled=True)
    parts = parts.reshape(n_x, n_zl, 2, quarter, ff).astype(jnp.float32)
    summed = jnp.sum(parts, axis=1)
    first = jnp.where(core == 0, summed[:, 0], summed[:, 1])
    second = jnp.where(core == 0, summed[:, 1], summed[:, 0])
    summed = jnp.stack([first, second], axis=0).reshape(act_rows, ff)
    kept = special[None, :] | (jnp.abs(activations.astype(jnp.float32)) <= 3.0)
    input_grad = jnp.where(kept, summed, 0.0).astype(jnp.bfloat16)
    return (input_grad, weight_grad)


def solution(mesh):
    fine = Mesh(mesh.devices.reshape(4, 4, 2, 4, 4), ("y", "zh", "c", "x", "zl"))
    dp, hidden = ("y", "zh", "c"), ("x", "zl")
    in_specs = (P(dp, hidden), P(hidden), P(dp, hidden), P(hidden, dp), P())
    out_specs = (P(hidden, dp), P(dp, hidden))
    return jax.shard_map(
        on_device, mesh=fine, in_specs=in_specs, out_specs=out_specs, check_vma=False
    )
```

time: 379 us -> 281 us (0.74)
  waiting for transfers between devices: 322 us -> 187 us
  blocking collectives: 0 us -> 42.5 us
  matrix products: 15.6 us -> 8.95 us
  other arithmetic: 4.35 us -> 8.43 us
    all_gather x2 -> x3, waiting for transfers between devices: 200 us -> 116 us  [the longest x1 39.5 us: on_device(): own = lax.all_gather(mine, 'y', axis=0, tiled=True)]
    reduce_scatter x1, waiting for transfers between devices: 98.3 us -> 36.8 us  [on_device(): wg = lax.psum_scatter(wg, 'x', scatter_dimension=0, tiled=True)]
    all_to_all x0 -> x2, blocking collectives: none -> 42.5 us  [the longest x1 33.9 us: on_device(): lax.all_to_all(spread, ('zh', 'zl'), split_axis=0, concat_axis=0, tiled=T...]
    all_to_all x0 -> x2, waiting for transfers between devices: none -> 33.8 us  [the longest x1 26.7 us: on_device(): lax.all_to_all(parts, ('x', 'zl'), split_axis=0, concat_axis=0, tiled=True)]
    ppermute x4 -> x1, waiting for transfers between devices: 23 us -> 0.01 us  [on_device(): other = lax.ppermute(own, 'c', [(0, 1), (1, 0)])]
    ppermute x4 -> x1, starting transfers between devices: 19.9 us -> 2.57 us  [on_device(): other = lax.ppermute(own, 'c', [(0, 1), (1, 0)])]
    all_to_all x0 -> x2, starting transfers between devices: none -> 15 us  [the longest x1 9.01 us: on_device(): lax.all_to_all(signed, ('x', 'zl'), split_axis=0, concat_axis=0, tiled=True)]
    dot_general x3 -> x5, matrix products: 15.6 us -> 8.95 us  [the longest x4 7.65 us: product(): lax.dot_general(a, b, (dims, ((), ())), preferred_element_type=jnp.float32)]
  transfers between devices with their start and end apart: 7 -> 7, of which waited for: 7 -> 6; matrix products, arithmetic and copies ran while one was open for 4% -> 1% of each run, Pallas kernels for 0% -> 0%
where the time goes in v1:
time: 281 us
  waiting for transfers between devices  187 us (67%)
  blocking collectives  42.5 us (15%)
  starting transfers between devices  17.7 us (6%)
  between operations  14 us (5%)
  matrix products  8.95 us (3%)
  other arithmetic  8.43 us (3%)
    all_gather x1, waiting for transfers between devices, on_device(): own = lax.all_gather(mine, 'y', axis=0, tiled=True)  39.5 us
    all_gather x1, waiting for transfers between devices, on_device(): weights = lax.all_gather(weight, 'x', axis=1, tiled=True)  38.1 us
    all_gather x1, waiting for transfers between devices, on_device(): acts = lax.all_gather(swapped, 'zl', axis=0, tiled=True)  38.1 us
    reduce_scatter x1, waiting for transfers between devices, on_device(): wg = lax.psum_scatter(wg, 'x', scatter_dimension=0, tiled=True)  36.8 us
    all_to_all x1, blocking collectives, on_device(): lax.all_to_all(spread, ('zh', 'zl'), split_axis=0, concat_axis=0, tiled=T...  33.9 us
    all_to_all x1, waiting for transfers between devices, on_device(): lax.all_to_all(parts, ('x', 'zl'), split_axis=0, concat_axis=0, tiled=True)  26.7 us
    all_to_all x1, starting transfers between devices, on_device(): lax.all_to_all(signed, ('x', 'zl'), split_axis=0, concat_axis=0, tiled=True)  9.01 us
    all_to_all x1, blocking collectives, on_device(): lax.all_to_all(clipped, 'x', split_axis=0, concat_axis=0, tiled=True)  8.59 us
  transfers between devices with their start and end apart: 7, of which 6 were waited for; matrix products, arithmetic and copies ran while one was open for 1% of the time, Pallas kernels for 0%

profile of v1, /device:TPU:1, one launch (start us, length us, event | category | flops | bytes accessed | tf_op | source)
XLA Modules:
  0.0 280.8 jit_solution(14088205078396384295)
XLA Ops:
  7.2 0.7 add_convert_fusion
  7.9 1.6 multiply_bitcast_fusion
  9.4 9.0 %all-to-all-start = ((bf16[16,8,512]{2,1,0:T(8,128)(2,1)}), bf16[16,8,512]{2,1,0:T(8,128)(2,1)S(1)}, u32[]{:S(2)}, u32[]{:S(2)}) async-start(bf16[16,8,512]{2,1,0:T(8,128)(2,1)} %multiply_bitcast_fusion), calls=%async_computation | async-start | bytes 262144 | tf_op jit(solution)/shard_map/all_to_all | solution.py:49
  18.4 0.0 all-gather.4.cloned.1.call-start
  18.5 7.1 %all-to-all-done = bf16[16,8,512]{2,1,0:T(8,128)(2,1)S(1)} async-done(((bf16[16,8,512]{2,1,0:T(8,128)(2,1)}), bf16[16,8,512]{2,1,0:T(8,128)(2,1)S(1)}, u32[]{:S(2)}, u32[]{:S(2)}) %all-to-all-start) | async-done | bytes 131104 | tf_op jit(solution)/shard_map/all_to_all | solution.py:49
  25.7 1.3 convolution_bitcast_fusion
  27.3 33.9 %all_to_all.42 = bf16[16,8,2048]{2,1,0:T(8,128)(2,1)} all-to-all(bf16[16,8,2048]{2,1,0:T(8,128)(2,1)S(1)} %bitcast.85), channel_id=1, replica_groups=mesh['y'=4,'zh'=4,'c'=2,'x'=4,'zl'=4] {'zh','zl'}, dimensions={0} | all-to-all | bytes 1048576 | tf_op jit(solution)/shard_map/all_to_all | solution.py:55
  61.2 0.0 all-gather.4.cloned.1.call-update
  61.2 0.0 all-gather.6.cloned.1.call-start
  61.3 0.7 all-gather.6.cloned.1.call-update
  62.0 39.5 %all-gather.4.cloned.1.call-done = bf16[512,2048]{1,0:T(8,128)(2,1)} async-done(((bf16[128,2048]{1,0:T(8,128)(2,1)}), bf16[512,2048]{1,0:T(8,128)(2,1)}) %all-gather.4.cloned.1.call-update) | async-done | bytes 2097168 | tf_op jit(solution)/shard_map/all_gather | solution.py:56
  101.5 2.6 collective-permute-start
  104.1 38.1 %all-gather.6.cloned.1.call-done = bf16[512,2048]{1,0:T(8,128)(2,1)} async-done(((bf16[512,512]{1,0:T(8,128)(2,1)}), bf16[512,2048]{1,0:T(8,128)(2,1)}) %all-gather.6.cloned.1.call-update) | async-done | bytes 2097168 | tf_op jit(solution)/shard_map/all_gather | solution.py:45
  142.2 3.6 %convolution_convert_fusion.1 = bf16[512,512]{1,0:T(8,128)(2,1)S(1)} fusion(bf16[512,2048]{1,0:T(8,128)(2,1)} %all-gather.4.cloned.1.call-done, bf16[512,2048]{1,0:T(8,128)(2,1)} %all-gather.6.cloned.1.call-done), kind=kOutput, calls=%fused_computation.7 | convolution fusion | flops 1074003968 | bytes 4718592 | tf_op jit(solution)/shard_map/dot_general | solution.py:74
  145.9 1.3 convolution_convert_fusion
  147.2 1.1 pad_maximum_fusion
  148.2 5.9 %all-to-all-start.2 = ((bf16[16,64,512]{2,1,0:T(8,128)(2,1)}), bf16[16,64,512]{2,1,0:T(8,128)(2,1)S(1)}, u32[]{:S(2)}, u32[]{:S(2)}) async-start(bf16[16,64,512]{2,1,0:T(8,128)(2,1)} %bitcast.19), calls=%async_computation.2 | async-start | bytes 2097152 | tf_op jit(solution)/shard_map/all_to_all | solution.py:86
  154.2 0.0 all-gather.8.cloned.1.call-start
  154.3 0.2 compare_reduce_fusion
  154.5 26.7 %all-to-all-done.2 = bf16[16,64,512]{2,1,0:T(8,128)(2,1)S(1)} async-done(((bf16[16,64,512]{2,1,0:T(8,128)(2,1)}), bf16[16,64,512]{2,1,0:T(8,128)(2,1)S(1)}, u32[]{:S(2)}, u32[]{:S(2)}) %all-to-all-start.2) | async-done | bytes 1048608 | tf_op jit(solution)/shard_map/all_to_all | solution.py:86
  181.2 0.2 convert_reduce_fusion
  181.5 0.9 clamp_select_fusion
  182.4 8.6 %all_to_all.43 = bf16[4,64,512]{2,1,0:T(8,128)(2,1)} all-to-all(bf16[4,64,512]{2,1,0:T(8,128)(2,1)S(1)} %bitcast.92), channel_id=1, replica_groups=mesh['y'=4,'zh'=4,'c'=2,'x'=4,'zl'=4] {'x'}, dimensions={0} | all-to-all | bytes 524288 | tf_op jit(solution)/shard_map/all_to_all | solution.py:66
  191.0 0.0 reduce-scatter.2.cloned.1.call-start
  191.1 38.1 %all-gather.8.cloned.1.call-done = bf16[1024,512]{1,0:T(8,128)(2,1)} async-done(((bf16[256,512]{1,0:T(8,128)(2,1)}), bf16[1024,512]{1,0:T(8,128)(2,1)}) %all-gather.8.cloned.1.call-update) | async-done | bytes 1048592 | tf_op jit(solution)/shard_map/all_gather | solution.py:67
  229.1 1.4 broadcast_select_fusion
  230.7 0.4 copy-done
  231.0 1.3 fusion.65
  232.3 1.4 multiply_convert_fusion
  233.8 1.5 copy.53
  235.3 36.8 %reduce-scatter.2.cloned.1.call-done = bf16[1,512,512]{2,1,0:T(8,128)(2,1)} async-done(((bf16[4,512,512]{2,1,0:T(8,128)(2,1)}), bf16[1,512,512]{2,1,0:T(8,128)(2,1)}) %reduce-scatter.2.cloned.1.call-update) | async-done | bytes 524304 | tf_op jit(solution)/shard_map/reduce_scatter | solution.py:78
  272.1 2.1 bitcast_convert_fusion
  (31 shorter events, 0.4 us)
Async XLA Ops:
  9.4 16.3 %all-to-all-start = ((bf16[16,8,512]{2,1,0:T(8,128)(2,1)}), bf16[16,8,512]{2,1,0:T(8,128)(2,1)S(1)}, u32[]{:S(2)}, u32[]{:S(2)}) async-start(bf16[16,8,512]{2,1,0:T(8,128)(2,1)} %multiply_bitcast_fusion), calls=%async_computation | async-start | bytes 262144 | tf_op jit(solution)/shard_map/all_to_all | solution.py:49
  18.4 83.0 %all-gather.4.cloned.1.call-start = ((), (), s32[]{:S(2)}) async-start(), calls=%async_computation.5 | async-start | bytes 2621440 | tf_op jit(solution)/shard_map/all_gather | solution.py:56
  61.2 81.0 %all-gather.6.cloned.1.call-start = ((), (), s32[]{:S(2)}) async-start(), calls=%async_computation.6 | async-start | bytes 2621440 | tf_op jit(solution)/shard_map/all_gather | solution.py:45
  101.5 44.4 %collective-permute-start = (bf16[512,2048]{1,0:T(8,128)(2,1)}, bf16[512,2048]{1,0:T(8,128)(2,1)S(1)}, u32[]{:S(2)}, u32[]{:S(2)}) collective-permute-start(bf16[512,2048]{1,0:T(8,128)(2,1)} %all-gather.4.cloned.1.call-done), channel_id=1, source_target_pairs={{0,16},{16,0},{1,17},{17,1},{2,18},{18,2},{3,19},{19,3},{4,20},{20... | collective-permute-start | bytes 6291464 | tf_op jit(solution)/shard_map/ppermute | solution.py:57
  142.2 3.7 %copy-start.3 = (bf16[512,2048]{1,0:T(8,128)(2,1)S(1)}, bf16[512,2048]{1,0:T(8,128)(2,1)}, u32[]{:S(2)}) copy-start(bf16[512,2048]{1,0:T(8,128)(2,1)} %all-gather.6.cloned.1.call-done) | copy-start | bytes 6291460
  147.2 7.1 %copy-start.2 = (s32[128]{0:T(128)S(1)}, s32[128]{0:T(128)}, u32[]{:S(2)}) copy-start(s32[128]{0:T(128)} %param.9) | copy-start | bytes 1540
  148.2 33.2 %copy-start.1 = (bf16[256,512]{1,0:T(8,128)(2,1)S(1)}, bf16[256,512]{1,0:T(8,128)(2,1)}, u32[]{:S(2)}) copy-start(bf16[256,512]{1,0:T(8,128)(2,1)} %param.8) | copy-start | bytes 786436
  148.2 33.0 %all-to-all-start.2 = ((bf16[16,64,512]{2,1,0:T(8,128)(2,1)}), bf16[16,64,512]{2,1,0:T(8,128)(2,1)S(1)}, u32[]{:S(2)}, u32[]{:S(2)}) async-start(bf16[16,64,512]{2,1,0:T(8,128)(2,1)} %bitcast.19), calls=%async_computation.2 | async-start | bytes 2097152 | tf_op jit(solution)/shard_map/all_to_all | solution.py:86
  154.2 74.9 %all-gather.8.cloned.1.call-start = ((), (), s32[]{:S(2)}) async-start(), calls=%async_computation.7 | async-start | bytes 1310720 | tf_op jit(solution)/shard_map/all_gather | solution.py:67
  191.0 81.1 %reduce-scatter.2.cloned.1.call-start = ((), (), s32[]{:S(2)}) async-start(), calls=%async_computation.8 | async-start | bytes 2621440 | tf_op jit(solution)/shard_map/reduce_scatter | solution.py:78
  229.1 1.9 copy-start
Sparse Core Ops, SparseCore 0:
  61.4 40.0 all-gather.3
  103.6 38.5 all-gather.5
  191.1 37.9 all-gather.7
  235.4 36.6 reduce-scatter.1

commit v2 on v1

--- a/solution.py
+++ b/solution.py
@@ -15,19 +15,23 @@
     return jnp.where(count % 2 == 0, 1.0, -1.0).astype(jnp.float32)
 
 
-def rotate_rows(rows, width):
-    groups = rows.shape[0] // 8
+def rotate_rows(rows, width, n_x, n_zl):
+    tokens = rows.shape[0] // (n_x * n_zl)
     local = jnp.dot(
         rows, hadamard_table(width).astype(jnp.bfloat16), preferred_element_type=jnp.float32
     )
-    local = local.reshape(groups, 8, width)
-    step = 1
-    while step < groups:
-        pairs = local.reshape(groups // (2 * step), 2, step, 8, width)
-        low, high = pairs[:, 0], pairs[:, 1]
-        local = jnp.stack([low + high, low - high], axis=1).reshape(groups, 8, width)
-        step *= 2
-    return local
+    local = local.reshape(n_x, n_zl, tokens, width)
+    both = jnp.bitwise_and(lax.axis_index("zl"), jnp.arange(n_zl, dtype=jnp.int32))
+    odd = jnp.bitwise_xor(both, both >> 1) & 1
+    local = jnp.sum(local * (1 - 2 * odd).astype(jnp.float32)[None, :, None, None], axis=1)
+    b0, b1, b2, b3 = (local[i] for i in range(n_x))
+    s0, d0, s1, d1 = b0 + b1, b0 - b1, b2 + b3, b2 - b3
+    return jnp.concatenate([s0 + s1, d0 + d1, s0 - s1, d0 - d1], axis=1)
+
+
+def shifted(array, axis, by):
+    n = lax.axis_size(axis)
+    return lax.ppermute(array, axis, [(i, (i + by) % n) for i in range(n)])
 
 
 def on_device(grad_out, signs, weight, activations, outliers):
@@ -35,7 +39,6 @@
     hidden = n_x * n_zl
     tok, width = grad_out.shape
     act_rows, ff = activations.shape
-    per = tok // hidden
     quarter = tok // n_x
     total = width * hidden
     factor = 1.0 / math.sqrt(total)
@@ -46,14 +49,20 @@
 
     flips = (2 * signs - 1).astype(jnp.bfloat16)
     signed = grad_out * flips[None, :]
-    rows = lax.all_to_all(signed, ("x", "zl"), split_axis=0, concat_axis=0, tiled=True)
-    rotated = (rotate_rows(rows, width) * factor).astype(jnp.bfloat16)
-    pieces = rotated.reshape(n_x, n_zl, per, width).transpose(1, 2, 0, 3)
-    pieces = pieces.reshape(n_zl, per, n_x * width)
-    spread = jnp.broadcast_to(pieces[None], (n_zh, n_zl, per, n_x * width))
-    spread = spread.reshape(n_zh * n_zl * per, n_x * width)
-    mine = lax.all_to_all(spread, ("zh", "zl"), split_axis=0, concat_axis=0, tiled=True)
-    own = lax.all_gather(mine, "y", axis=0, tiled=True)
+    spread = jnp.broadcast_to(
+        signed.reshape(n_x, 1, quarter, width), (n_x, n_zl, quarter, width)
+    ).reshape(hidden * quarter, width)
+    rows = lax.all_to_all(spread, ("x", "zl"), split_axis=0, concat_axis=0, tiled=True)
+    mine = (rotate_rows(rows, width, n_x, n_zl) * factor).astype(jnp.bfloat16)
+    y, zh = lax.axis_index("y"), lax.axis_index("zh")
+    own = jnp.zeros((n_y, n_zh, quarter, n_x * width), jnp.bfloat16)
+    for k in range(n_zh):
+        block = shifted(mine, "zh", k) if k else mine
+        for j in range(n_y):
+            piece = shifted(block, "y", j) if j else block
+            place = ((y + n_y - j) % n_y, (zh + n_zh - k) % n_zh, 0, 0)
+            own = lax.dynamic_update_slice(own, piece[None, None], place)
+    own = own.reshape(hidden * quarter, n_x * width)
     other = lax.ppermute(own, "c", [(0, 1), (1, 0)])
 
     channel = (

time: 281 us -> 257 us (0.915)
  starting transfers between devices: 17.7 us -> 79.8 us
  waiting for transfers between devices: 187 us -> 131 us
  blocking collectives: 42.5 us -> 8.58 us
    ppermute x0 -> x15, starting transfers between devices: none -> 55.6 us  [shifted(): return lax.ppermute(array, axis, [(i, (i + by) % n) for i in range(n)])]
    all_gather x1 -> x0, waiting for transfers between devices: 39.5 us -> none  [on_device(): own = lax.all_gather(mine, 'y', axis=0, tiled=True)]
    all_gather x1, waiting for transfers between devices: 38.1 us -> 0.02 us  [on_device(): weights = lax.all_gather(weight, 'x', axis=1, tiled=True)]
    all_to_all x1 -> x0, blocking collectives: 33.9 us -> none  [on_device(): lax.all_to_all(spread, ('zh', 'zl'), split_axis=0, concat_axis=0, tiled=T...]
    ppermute x0 -> x15, waiting for transfers between devices: none -> 19.4 us  [shifted(): return lax.ppermute(array, axis, [(i, (i + by) % n) for i in range(n)])]
    ppermute x1, starting transfers between devices: 2.57 us -> 11.3 us  [on_device(): other = lax.ppermute(own, 'c', [(0, 1), (1, 0)])]
    all_to_all x1, waiting for transfers between devices: 7.15 us -> 14.8 us  [on_device(): lax.all_to_all(spread, ('x', 'zl'), split_axis=0, concat_axis=0, tiled=True)]
    all_gather x1, waiting for transfers between devices: 38.1 us -> 31.9 us  [on_device(): acts = lax.all_gather(swapped, 'zl', axis=0, tiled=True)]
  transfers between devices with their start and end apart: 7 -> 21, of which waited for: 6 -> 11; matrix products, arithmetic and copies ran while one was open for 1% -> 2% of each run, Pallas kernels for 0% -> 0%
where the time goes in v2:
time: 257 us; the launch traced here: 256 us
  waiting for transfers between devices  131 us (51%)
  starting transfers between devices  79.8 us (31%)
  between operations  14.4 us (6%)
  matrix products  11.7 us (5%)
  blocking collectives  8.58 us (3%)
  other arithmetic  7.61 us (3%)
  local copies, waits for them, and re-layouts  2.95 us (1%)
    ppermute x15, starting transfers between devices, shifted(): return lax.ppermute(array, axis, [(i, (i + by) % n) for i in range(n)])  55.6 us
    reduce_scatter x1, waiting for transfers between devices, on_device(): wg = lax.psum_scatter(wg, 'x', scatter_dimension=0, tiled=True)  36.8 us
    all_gather x1, waiting for transfers between devices, on_device(): acts = lax.all_gather(swapped, 'zl', axis=0, tiled=True)  31.9 us
    all_to_all x1, waiting for transfers between devices, on_device(): lax.all_to_all(parts, ('x', 'zl'), split_axis=0, concat_axis=0, tiled=True)  26.7 us
    ppermute x15, waiting for transfers between devices, shifted(): return lax.ppermute(array, axis, [(i, (i + by) % n) for i in range(n)])  19.4 us
    all_to_all x1, waiting for transfers between devices, on_device(): lax.all_to_all(spread, ('x', 'zl'), split_axis=0, concat_axis=0, tiled=True)  14.8 us
    ppermute x1, starting transfers between devices, on_device(): other = lax.ppermute(own, 'c', [(0, 1), (1, 0)])  11.3 us
    dot_general x4, matrix products, product(): lax.dot_general(a, b, (dims, ((), ())), preferred_element_type=jnp.float32)  10.2 us
  transfers between devices with their start and end apart: 21, of which 11 were waited for; matrix products, arithmetic and copies ran while one was open for 2% of the time, Pallas kernels for 0%

profile of v2, /device:TPU:1, one launch (start us, length us, event | category | flops | bytes accessed | tf_op | source)
XLA Modules:
  0.0 256.2 jit_solution(16664391386356210525)
XLA Ops:
  9.6 9.0 %all-to-all-start = ((bf16[16,32,512]{2,1,0:T(8,128)(2,1)}), bf16[16,32,512]{2,1,0:T(8,128)(2,1)S(1)}, u32[]{:S(2)}, u32[]{:S(2)}) async-start(bf16[16,32,512]{2,1,0:T(8,128)(2,1)} %bitcast.1), calls=%async_computation | async-start | bytes 1048576 | tf_op jit(solution)/shard_map/all_to_all | solution.py:55
  19.6 14.8 %all-to-all-done = bf16[16,32,512]{2,1,0:T(8,128)(2,1)S(1)} async-done(((bf16[16,32,512]{2,1,0:T(8,128)(2,1)}), bf16[16,32,512]{2,1,0:T(8,128)(2,1)S(1)}, u32[]{:S(2)}, u32[]{:S(2)}) %all-to-all-start) | async-done | bytes 524320 | tf_op jit(solution)/shard_map/all_to_all | solution.py:55
  35.9 9.8 %collective-permute-start.11 = (bf16[32,2048]{1,0:T(8,128)(2,1)S(1)}, bf16[32,2048]{1,0:T(8,128)(2,1)S(1)}, u32[]{:S(2)}, u32[]{:S(2)}) collective-permute-start(bf16[32,2048]{1,0:T(8,128)(2,1)S(1)} %fusion.31), channel_id=1, source_target_pairs={{0,96},{32,0},{64,32},{96,64},{1,97},{33,1},{65,33},{97,65},{2,98}... | collective-permute-start | bytes 393224 | tf_op jit(solution)/shard_map/ppermute | solution.py:34
  45.7 6.1 %collective-permute-start.7 = (bf16[32,2048]{1,0:T(8,128)(2,1)S(1)}, bf16[32,2048]{1,0:T(8,128)(2,1)S(1)}, u32[]{:S(2)}, u32[]{:S(2)}) collective-permute-start(bf16[32,2048]{1,0:T(8,128)(2,1)S(1)} %fusion.31), channel_id=1, source_target_pairs={{0,64},{32,96},{64,0},{96,32},{1,65},{33,97},{65,1},{97,33},{2,66}... | collective-permute-start | bytes 393224 | tf_op jit(solution)/shard_map/ppermute | solution.py:34
  51.8 6.1 %collective-permute-start.3 = (bf16[32,2048]{1,0:T(8,128)(2,1)S(1)}, bf16[32,2048]{1,0:T(8,128)(2,1)S(1)}, u32[]{:S(2)}, u32[]{:S(2)}) collective-permute-start(bf16[32,2048]{1,0:T(8,128)(2,1)S(1)} %fusion.31), channel_id=1, source_target_pairs={{0,32},{32,64},{64,96},{96,0},{1,33},{33,65},{65,97},{97,1},{2,34}... | collective-permute-start | bytes 393224 | tf_op jit(solution)/shard_map/ppermute | solution.py:34
  57.9 4.6 %collective-permute-start.2 = (bf16[32,2048]{1,0:T(8,128)(2,1)S(1)}, bf16[32,2048]{1,0:T(8,128)(2,1)S(1)}, u32[]{:S(2)}, u32[]{:S(2)}) collective-permute-start(bf16[32,2048]{1,0:T(8,128)(2,1)S(1)} %fusion.31), channel_id=1, source_target_pairs={{0,384},{128,0},{256,128},{384,256},{1,385},{129,1},{257,129},{385... | collective-permute-start | bytes 393224 | tf_op jit(solution)/shard_map/ppermute | solution.py:34
  62.6 1.9 collective-permute-start
  64.8 3.5 %collective-permute-start.1 = (bf16[32,2048]{1,0:T(8,128)(2,1)S(1)}, bf16[32,2048]{1,0:T(8,128)(2,1)S(1)}, u32[]{:S(2)}, u32[]{:S(2)}) collective-permute-start(bf16[32,2048]{1,0:T(8,128)(2,1)S(1)} %fusion.31), channel_id=1, source_target_pairs={{0,256},{128,384},{256,0},{384,128},{1,257},{129,385},{257,1},{385... | collective-permute-start | bytes 393224 | tf_op jit(solution)/shard_map/ppermute | solution.py:34
  69.8 1.9 collective-permute-start.14
  71.7 1.8 collective-permute-done.1
  73.5 3.0 %collective-permute-start.13 = (bf16[32,2048]{1,0:T(8,128)(2,1)S(1)}, bf16[32,2048]{1,0:T(8,128)(2,1)S(1)}, u32[]{:S(2)}, u32[]{:S(2)}) collective-permute-start(bf16[32,2048]{1,0:T(8,128)(2,1)S(1)} %collective-permute-done.11), channel_id=1, source_target_pairs={{0,256},{128,384},{256,0},{384,128},{1,257},{129,385},{257,1},{385... | collective-permute-start | bytes 393224 | tf_op jit(solution)/shard_map/ppermute | solution.py:34
  76.5 2.9 %collective-permute-start.12 = (bf16[32,2048]{1,0:T(8,128)(2,1)S(1)}, bf16[32,2048]{1,0:T(8,128)(2,1)S(1)}, u32[]{:S(2)}, u32[]{:S(2)}) collective-permute-start(bf16[32,2048]{1,0:T(8,128)(2,1)S(1)} %collective-permute-done.11), channel_id=1, source_target_pairs={{0,128},{128,256},{256,384},{384,0},{1,129},{129,257},{257,385},{3... | collective-permute-start | bytes 393224 | tf_op jit(solution)/shard_map/ppermute | solution.py:34
  79.4 2.5 collective-permute-start.4
  82.0 4.8 %collective-permute-done.4 = bf16[32,2048]{1,0:T(8,128)(2,1)S(1)} collective-permute-done((bf16[32,2048]{1,0:T(8,128)(2,1)S(1)}, bf16[32,2048]{1,0:T(8,128)(2,1)S(1)}, u32[]{:S(2)}, u32[]{:S(2)}) %collective-permute-start.4) | collective-permute-done | bytes 131104 | tf_op jit(solution)/shard_map/ppermute | solution.py:34
  86.8 2.5 collective-permute-start.5
  89.3 3.1 %collective-permute-start.6 = (bf16[32,2048]{1,0:T(8,128)(2,1)S(1)}, bf16[32,2048]{1,0:T(8,128)(2,1)S(1)}, u32[]{:S(2)}, u32[]{:S(2)}) collective-permute-start(bf16[32,2048]{1,0:T(8,128)(2,1)S(1)} %collective-permute-done.3), channel_id=1, source_target_pairs={{0,384},{128,0},{256,128},{384,256},{1,385},{129,1},{257,129},{385... | collective-permute-start | bytes 393224 | tf_op jit(solution)/shard_map/ppermute | solution.py:34
  92.4 1.6 collective-permute-done.5
  94.0 2.2 collective-permute-start.10
  96.2 3.1 %collective-permute-start.8 = (bf16[32,2048]{1,0:T(8,128)(2,1)S(1)}, bf16[32,2048]{1,0:T(8,128)(2,1)S(1)}, u32[]{:S(2)}, u32[]{:S(2)}) collective-permute-start(bf16[32,2048]{1,0:T(8,128)(2,1)S(1)} %collective-permute-done.7), channel_id=1, source_target_pairs={{0,128},{128,256},{256,384},{384,0},{1,129},{129,257},{257,385},{3... | collective-permute-start | bytes 393224 | tf_op jit(solution)/shard_map/ppermute | solution.py:34
  99.4 3.8 %collective-permute-done.8 = bf16[32,2048]{1,0:T(8,128)(2,1)S(1)} collective-permute-done((bf16[32,2048]{1,0:T(8,128)(2,1)S(1)}, bf16[32,2048]{1,0:T(8,128)(2,1)S(1)}, u32[]{:S(2)}, u32[]{:S(2)}) %collective-permute-start.8) | collective-permute-done | bytes 131104 | tf_op jit(solution)/shard_map/ppermute | solution.py:34
  103.1 2.5 collective-permute-start.9
  105.7 6.0 %collective-permute-done.9 = bf16[32,2048]{1,0:T(8,128)(2,1)S(1)} collective-permute-done((bf16[32,2048]{1,0:T(8,128)(2,1)S(1)}, bf16[32,2048]{1,0:T(8,128)(2,1)S(1)}, u32[]{:S(2)}, u32[]{:S(2)}) %collective-permute-start.9) | collective-permute-done | bytes 131104 | tf_op jit(solution)/shard_map/ppermute | solution.py:34
  111.8 11.3 %collective-permute-start.15 = (bf16[512,2048]{1,0:T(8,128)(2,1)S(1)}, bf16[512,2048]{1,0:T(8,128)(2,1)}, u32[]{:S(2)}, u32[]{:S(2)}) collective-permute-start(bf16[512,2048]{1,0:T(8,128)(2,1)S(1)} %bitcast.113), channel_id=1, source_target_pairs={{0,16},{16,0},{1,17},{17,1},{2,18},{18,2},{3,19},{19,3},{4,20},{20... | collective-permute-start | bytes 6291464 | tf_op jit(solution)/shard_map/ppermute | solution.py:66
  123.1 3.0 %convolution_convert_fusion.1 = bf16[512,512]{1,0:T(8,128)(2,1)S(1)} fusion(bf16[512,2048]{1,0:T(8,128)(2,1)S(1)} %bitcast.114, bf16[512,2048]{1,0:T(8,128)(2,1)} %all-gather.3.cloned.1.call-done), kind=kOutput, calls=%fused_computation.8 | convolution fusion | flops 1074003968 | bytes 4718592 | tf_op jit(solution)/shard_map/dot_general | solution.py:83
  127.0 2.9 %convolution_convert_fusion = bf16[512,512]{1,0:T(8,128)(2,1)S(1)} fusion(bf16[512,2048]{1,0:T(8,128)(2,1)} %collective-permute-done.15, bf16[512,2048]{1,0:T(8,128)(2,1)S(1)} %copy-done.2), kind=kOutput, calls=%fused_computation.7 | convolution fusion | flops 1074003968 | bytes 4718592 | tf_op jit(solution)/shard_map/dot_general | solution.py:83
  131.0 3.8 %all-to-all-start.1 = ((bf16[16,64,512]{2,1,0:T(8,128)(2,1)}), bf16[16,64,512]{2,1,0:T(8,128)(2,1)S(1)}, u32[]{:S(2)}, u32[]{:S(2)}) async-start(bf16[16,64,512]{2,1,0:T(8,128)(2,1)} %bitcast.117), calls=%async_computation.1 | async-start | bytes 2097152 | tf_op jit(solution)/shard_map/all_to_all | solution.py:95
  135.1 26.7 %all-to-all-done.1 = bf16[16,64,512]{2,1,0:T(8,128)(2,1)S(1)} async-done(((bf16[16,64,512]{2,1,0:T(8,128)(2,1)}), bf16[16,64,512]{2,1,0:T(8,128)(2,1)S(1)}, u32[]{:S(2)}, u32[]{:S(2)}) %all-to-all-start.1) | async-done | bytes 1048608 | tf_op jit(solution)/shard_map/all_to_all | solution.py:95
  163.0 8.6 %all_to_all.30 = bf16[4,64,512]{2,1,0:T(8,128)(2,1)} all-to-all(bf16[4,64,512]{2,1,0:T(8,128)(2,1)S(1)} %bitcast.122), channel_id=1, replica_groups=mesh['y'=4,'zh'=4,'c'=2,'x'=4,'zl'=4] {'x'}, dimensions={0} | all-to-all | bytes 524288 | tf_op jit(solution)/shard_map/all_to_all | solution.py:75
  171.6 31.9 %all-gather.5.cloned.1.call-done = bf16[1024,512]{1,0:T(8,128)(2,1)} async-done(((bf16[256,512]{1,0:T(8,128)(2,1)}), bf16[1024,512]{1,0:T(8,128)(2,1)}) %all-gather.5.cloned.1.call-update) | async-done | bytes 1048592 | tf_op jit(solution)/shard_map/all_gather | solution.py:76
  204.9 2.9 %fusion.69 = f32[512,2048]{1,0:T(8,128)S(1)} fusion(bf16[512,512]{1,0:T(8,128)(2,1)S(1)} %bitcast.119, bf16[512,2048]{1,0:T(8,128)(2,1)} %collective-permute-done.15), kind=kOutput, calls=%fused_computation.172 | convolution fusion | flops 1073741824 | bytes 6815744 | tf_op jit(solution)/shard_map/dot_general | solution.py:83
  210.7 36.8 %reduce-scatter.2.cloned.1.call-done = bf16[1,512,512]{2,1,0:T(8,128)(2,1)} async-done(((bf16[4,512,512]{2,1,0:T(8,128)(2,1)}), bf16[1,512,512]{2,1,0:T(8,128)(2,1)}) %reduce-scatter.2.cloned.1.call-update) | async-done | bytes 524304 | tf_op jit(solution)/shard_map/reduce_scatter | solution.py:87
  247.5 2.1 bitcast_convert_fusion
  (69 shorter events, 14.5 us)
Async XLA Ops:
  9.6 24.7 %all-to-all-start = ((bf16[16,32,512]{2,1,0:T(8,128)(2,1)}), bf16[16,32,512]{2,1,0:T(8,128)(2,1)S(1)}, u32[]{:S(2)}, u32[]{:S(2)}) async-start(bf16[16,32,512]{2,1,0:T(8,128)(2,1)} %bitcast.1), calls=%async_computation | async-start | bytes 1048576 | tf_op jit(solution)/shard_map/all_to_all | solution.py:55
  18.6 104.5 %all-gather.3.cloned.1.call-start = ((), (), s32[]{:S(2)}) async-start(), calls=%async_computation.4 | async-start | bytes 2621440 | tf_op jit(solution)/shard_map/all_gather | solution.py:48
  35.9 28.8 %collective-permute-start.11 = (bf16[32,2048]{1,0:T(8,128)(2,1)S(1)}, bf16[32,2048]{1,0:T(8,128)(2,1)S(1)}, u32[]{:S(2)}, u32[]{:S(2)}) collective-permute-start(bf16[32,2048]{1,0:T(8,128)(2,1)S(1)} %fusion.31), channel_id=1, source_target_pairs={{0,96},{32,0},{64,32},{96,64},{1,97},{33,1},{65,33},{97,65},{2,98}... | collective-permute-start | bytes 393224 | tf_op jit(solution)/shard_map/ppermute | solution.py:34
  45.7 43.6 %collective-permute-start.7 = (bf16[32,2048]{1,0:T(8,128)(2,1)S(1)}, bf16[32,2048]{1,0:T(8,128)(2,1)S(1)}, u32[]{:S(2)}, u32[]{:S(2)}) collective-permute-start(bf16[32,2048]{1,0:T(8,128)(2,1)S(1)} %fusion.31), channel_id=1, source_target_pairs={{0,64},{32,96},{64,0},{96,32},{1,65},{33,97},{65,1},{97,33},{2,66}... | collective-permute-start | bytes 393224 | tf_op jit(solution)/shard_map/ppermute | solution.py:34
  51.8 24.7 %collective-permute-start.3 = (bf16[32,2048]{1,0:T(8,128)(2,1)S(1)}, bf16[32,2048]{1,0:T(8,128)(2,1)S(1)}, u32[]{:S(2)}, u32[]{:S(2)}) collective-permute-start(bf16[32,2048]{1,0:T(8,128)(2,1)S(1)} %fusion.31), channel_id=1, source_target_pairs={{0,32},{32,64},{64,96},{96,0},{1,33},{33,65},{65,97},{97,1},{2,34}... | collective-permute-start | bytes 393224 | tf_op jit(solution)/shard_map/ppermute | solution.py:34
  57.9 21.5 %collective-permute-start.2 = (bf16[32,2048]{1,0:T(8,128)(2,1)S(1)}, bf16[32,2048]{1,0:T(8,128)(2,1)S(1)}, u32[]{:S(2)}, u32[]{:S(2)}) collective-permute-start(bf16[32,2048]{1,0:T(8,128)(2,1)S(1)} %fusion.31), channel_id=1, source_target_pairs={{0,384},{128,0},{256,128},{384,256},{1,385},{129,1},{257,129},{385... | collective-permute-start | bytes 393224 | tf_op jit(solution)/shard_map/ppermute | solution.py:34
  62.6 7.2 %collective-permute-start = (bf16[32,2048]{1,0:T(8,128)(2,1)S(1)}, bf16[32,2048]{1,0:T(8,128)(2,1)S(1)}, u32[]{:S(2)}, u32[]{:S(2)}) collective-permute-start(bf16[32,2048]{1,0:T(8,128)(2,1)S(1)} %fusion.31), channel_id=1, source_target_pairs={{0,128},{128,256},{256,384},{384,0},{1,129},{129,257},{257,385},{3... | collective-permute-start | bytes 393224 | tf_op jit(solution)/shard_map/ppermute | solution.py:34
  64.8 8.7 %collective-permute-start.1 = (bf16[32,2048]{1,0:T(8,128)(2,1)S(1)}, bf16[32,2048]{1,0:T(8,128)(2,1)S(1)}, u32[]{:S(2)}, u32[]{:S(2)}) collective-permute-start(bf16[32,2048]{1,0:T(8,128)(2,1)S(1)} %fusion.31), channel_id=1, source_target_pairs={{0,256},{128,384},{256,0},{384,128},{1,257},{129,385},{257,1},{385... | collective-permute-start | bytes 393224 | tf_op jit(solution)/shard_map/ppermute | solution.py:34
  69.8 42.0 %collective-permute-start.14 = (bf16[32,2048]{1,0:T(8,128)(2,1)S(1)}, bf16[32,2048]{1,0:T(8,128)(2,1)S(1)}, u32[]{:S(2)}, u32[]{:S(2)}) collective-permute-start(bf16[32,2048]{1,0:T(8,128)(2,1)S(1)} %collective-permute-done.11), channel_id=1, source_target_pairs={{0,384},{128,0},{256,128},{384,256},{1,385},{129,1},{257,129},{385... | collective-permute-start | bytes 393224 | tf_op jit(solution)/shard_map/ppermute | solution.py:34
  73.5 38.3 %collective-permute-start.13 = (bf16[32,2048]{1,0:T(8,128)(2,1)S(1)}, bf16[32,2048]{1,0:T(8,128)(2,1)S(1)}, u32[]{:S(2)}, u32[]{:S(2)}) collective-permute-start(bf16[32,2048]{1,0:T(8,128)(2,1)S(1)} %collective-permute-done.11), channel_id=1, source_target_pairs={{0,256},{128,384},{256,0},{384,128},{1,257},{129,385},{257,1},{385... | collective-permute-start | bytes 393224 | tf_op jit(solution)/shard_map/ppermute | solution.py:34
  76.5 35.2 %collective-permute-start.12 = (bf16[32,2048]{1,0:T(8,128)(2,1)S(1)}, bf16[32,2048]{1,0:T(8,128)(2,1)S(1)}, u32[]{:S(2)}, u32[]{:S(2)}) collective-permute-start(bf16[32,2048]{1,0:T(8,128)(2,1)S(1)} %collective-permute-done.11), channel_id=1, source_target_pairs={{0,128},{128,256},{256,384},{384,0},{1,129},{129,257},{257,385},{3... | collective-permute-start | bytes 393224 | tf_op jit(solution)/shard_map/ppermute | solution.py:34
  79.4 7.4 %collective-permute-start.4 = (bf16[32,2048]{1,0:T(8,128)(2,1)S(1)}, bf16[32,2048]{1,0:T(8,128)(2,1)S(1)}, u32[]{:S(2)}, u32[]{:S(2)}) collective-permute-start(bf16[32,2048]{1,0:T(8,128)(2,1)S(1)} %collective-permute-done.3), channel_id=1, source_target_pairs={{0,128},{128,256},{256,384},{384,0},{1,129},{129,257},{257,385},{3... | collective-permute-start | bytes 393224 | tf_op jit(solution)/shard_map/ppermute | solution.py:34
  86.8 7.2 %collective-permute-start.5 = (bf16[32,2048]{1,0:T(8,128)(2,1)S(1)}, bf16[32,2048]{1,0:T(8,128)(2,1)S(1)}, u32[]{:S(2)}, u32[]{:S(2)}) collective-permute-start(bf16[32,2048]{1,0:T(8,128)(2,1)S(1)} %collective-permute-done.3), channel_id=1, source_target_pairs={{0,256},{128,384},{256,0},{384,128},{1,257},{129,385},{257,1},{385... | collective-permute-start | bytes 393224 | tf_op jit(solution)/shard_map/ppermute | solution.py:34
  89.3 6.9 %collective-permute-start.6 = (bf16[32,2048]{1,0:T(8,128)(2,1)S(1)}, bf16[32,2048]{1,0:T(8,128)(2,1)S(1)}, u32[]{:S(2)}, u32[]{:S(2)}) collective-permute-start(bf16[32,2048]{1,0:T(8,128)(2,1)S(1)} %collective-permute-done.3), channel_id=1, source_target_pairs={{0,384},{128,0},{256,128},{384,256},{1,385},{129,1},{257,129},{385... | collective-permute-start | bytes 393224 | tf_op jit(solution)/shard_map/ppermute | solution.py:34
  94.0 17.7 %collective-permute-start.10 = (bf16[32,2048]{1,0:T(8,128)(2,1)S(1)}, bf16[32,2048]{1,0:T(8,128)(2,1)S(1)}, u32[]{:S(2)}, u32[]{:S(2)}) collective-permute-start(bf16[32,2048]{1,0:T(8,128)(2,1)S(1)} %collective-permute-done.7), channel_id=1, source_target_pairs={{0,384},{128,0},{256,128},{384,256},{1,385},{129,1},{257,129},{385... | collective-permute-start | bytes 393224 | tf_op jit(solution)/shard_map/ppermute | solution.py:34
  96.2 6.9 %collective-permute-start.8 = (bf16[32,2048]{1,0:T(8,128)(2,1)S(1)}, bf16[32,2048]{1,0:T(8,128)(2,1)S(1)}, u32[]{:S(2)}, u32[]{:S(2)}) collective-permute-start(bf16[32,2048]{1,0:T(8,128)(2,1)S(1)} %collective-permute-done.7), channel_id=1, source_target_pairs={{0,128},{128,256},{256,384},{384,0},{1,129},{129,257},{257,385},{3... | collective-permute-start | bytes 393224 | tf_op jit(solution)/shard_map/ppermute | solution.py:34
  103.1 8.5 %collective-permute-start.9 = (bf16[32,2048]{1,0:T(8,128)(2,1)S(1)}, bf16[32,2048]{1,0:T(8,128)(2,1)S(1)}, u32[]{:S(2)}, u32[]{:S(2)}) collective-permute-start(bf16[32,2048]{1,0:T(8,128)(2,1)S(1)} %collective-permute-done.7), channel_id=1, source_target_pairs={{0,256},{128,384},{256,0},{384,128},{1,257},{129,385},{257,1},{385... | collective-permute-start | bytes 393224 | tf_op jit(solution)/shard_map/ppermute | solution.py:34
  111.8 15.2 %collective-permute-start.15 = (bf16[512,2048]{1,0:T(8,128)(2,1)S(1)}, bf16[512,2048]{1,0:T(8,128)(2,1)}, u32[]{:S(2)}, u32[]{:S(2)}) collective-permute-start(bf16[512,2048]{1,0:T(8,128)(2,1)S(1)} %bitcast.113), channel_id=1, source_target_pairs={{0,16},{16,0},{1,17},{17,1},{2,18},{18,2},{3,19},{19,3},{4,20},{20... | collective-permute-start | bytes 6291464 | tf_op jit(solution)/shard_map/ppermute | solution.py:66
  123.1 3.9 %copy-start.2 = (bf16[512,2048]{1,0:T(8,128)(2,1)S(1)}, bf16[512,2048]{1,0:T(8,128)(2,1)}, u32[]{:S(2)}) copy-start(bf16[512,2048]{1,0:T(8,128)(2,1)} %all-gather.3.cloned.1.call-done) | copy-start | bytes 6291460
  129.9 5.0 %copy-start.1 = (s32[128]{0:T(128)S(1)}, s32[128]{0:T(128)}, u32[]{:S(2)}) copy-start(s32[128]{0:T(128)} %param.9) | copy-start | bytes 1540
  131.0 31.1 %copy-start = (bf16[256,512]{1,0:T(8,128)(2,1)S(1)}, bf16[256,512]{1,0:T(8,128)(2,1)}, u32[]{:S(2)}) copy-start(bf16[256,512]{1,0:T(8,128)(2,1)} %param.8) | copy-start | bytes 786436
  131.0 30.8 %all-to-all-start.1 = ((bf16[16,64,512]{2,1,0:T(8,128)(2,1)}), bf16[16,64,512]{2,1,0:T(8,128)(2,1)S(1)}, u32[]{:S(2)}, u32[]{:S(2)}) async-start(bf16[16,64,512]{2,1,0:T(8,128)(2,1)} %bitcast.117), calls=%async_computation.1 | async-start | bytes 2097152 | tf_op jit(solution)/shard_map/all_to_all | solution.py:95
  134.8 68.7 %all-gather.5.cloned.1.call-start = ((), (), s32[]{:S(2)}) async-start(), calls=%async_computation.5 | async-start | bytes 1310720 | tf_op jit(solution)/shard_map/all_gather | solution.py:76
  171.6 76.0 %reduce-scatter.2.cloned.1.call-start = ((), (), s32[]{:S(2)}) async-start(), calls=%async_computation.6 | async-start | bytes 2621440 | tf_op jit(solution)/shard_map/reduce_scatter | solution.py:87
Sparse Core Ops, SparseCore 0:
  21.6 40.9 all-gather.2
  171.7 31.7 all-gather.4
  210.8 36.6 reduce-scatter.1

commit v3 on v2

v3 whole, which is shorter than its diff:
```python
import math

import jax
import jax.numpy as jnp
from jax import lax
from jax.experimental import pallas as pl
from jax.experimental.pallas import tpu as pltpu
from jax.sharding import Mesh, PartitionSpec as P


def hadamard_table(order):
    index = jnp.arange(order, dtype=jnp.int32)
    count = jnp.zeros((order, order), jnp.int32)
    for level in range(order.bit_length() - 1):
        step = 2**level
        count = count + index[:, None] // step % 2 * (index[None, :] // step % 2)
    return jnp.where(count % 2 == 0, 1.0, -1.0).astype(jnp.float32)


def parity_signs(a, b):
    both = jnp.bitwise_and(a, b)
    return (1 - 2 * (jnp.bitwise_xor(both, both >> 1) & 1)).astype(jnp.float32)


def rotate_rows(rows, width, n_x, n_zl):
    tokens = rows.shape[0] // (n_x * n_zl)
    local = jnp.dot(
        rows, hadamard_table(width).astype(jnp.bfloat16), preferred_element_type=jnp.float32
    )
    local = local.reshape(n_x, n_zl, tokens, width)
    every = jnp.arange(n_zl, dtype=jnp.int32)
    local = jnp.sum(
        local * parity_signs(lax.axis_index("zl"), every)[None, :, None, None], axis=1
    )
    b0, b1, b2, b3 = (local[i] for i in range(n_x))
    s0, d0, s1, d1 = b0 + b1, b0 - b1, b2 + b3, b2 - b3
    return jnp.concatenate([s0 + s1, d0 + d1, s0 - s1, d0 - d1], axis=1)


def shifted(array, axis, by):
    n = lax.axis_size(axis)
    return lax.ppermute(array, axis, [(i, (i + by) % n) for i in range(n)])


def picked(array, index):
    return lax.dynamic_index_in_dim(array, index, 0, keepdims=False)


def exchanged(pieces, axis):
    n = lax.axis_size(axis)
    me = lax.axis_index(axis)
    came = pieces
    for by in range(1, n):
        piece = shifted(picked(pieces, (me + by) % n), axis, by)
        came = lax.dynamic_update_slice_in_dim(came, piece[None], (me + n - by) % n, 0)
    return came


def spread_over(array, axis):
    n = lax.axis_size(axis)
    copies = jnp.broadcast_to(array[None], (n,) + array.shape)
    return lax.all_to_all(copies, axis, split_axis=0, concat_axis=0, tiled=True)


def weight_kernel(scale, core_ref, acts_ref, own_ref, other_ref, out_ref, rows_ref, turned_ref):
    tokens = own_ref.shape[0]
    n_zl, n_x, _, quarter, _ = acts_ref.shape

    @pl.when(pl.program_id(0) == 0)
    def _():
        for half in range(2):
            core = jnp.bitwise_xor(core_ref[0], half)
            for i in range(n_x):
                for j in range(n_zl):
                    at = half * tokens + (i * n_zl + j) * quarter
                    rows_ref[at : at + quarter, :] = acts_ref[j, i, core]
        turned_ref[...] = rows_ref[...].T

    part = jnp.dot(turned_ref[:, :tokens], own_ref[...], preferred_element_type=jnp.float32)
    part += jnp.dot(turned_ref[:, tokens:], other_ref[...], preferred_element_type=jnp.float32)
    out_ref[0] = (part * scale).astype(out_ref.dtype)


def weight_product(core, acts, own, other, width, scale):
    ff = acts.shape[-1]
    tokens, wide = own.shape
    blocks = wide // width
    block = pl.BlockSpec((tokens, width), lambda i: (0, i))
    return pl.pallas_call(
        lambda *refs: weight_kernel(scale, *refs),
        grid=(blocks,),
        in_specs=[
            pl.BlockSpec(memory_space=pltpu.SMEM),
            pl.BlockSpec(acts.shape, lambda i: (0, 0, 0, 0, 0)),
            block,
            block,
        ],
        out_specs=pl.BlockSpec((1, ff, width), lambda i: (i, 0, 0)),
        out_shape=jax.ShapeDtypeStruct((blocks, ff, width), jnp.bfloat16),
        scratch_shapes=[
            pltpu.VMEM((2 * tokens, ff), jnp.bfloat16),
            pltpu.VMEM((ff, 2 * tokens), jnp.bfloat16),
        ],
        compiler_params=pltpu.CompilerParams(vmem_limit_bytes=14 * 2**20),
        cost_estimate=pl.CostEstimate(
            flops=4 * ff * tokens * wide, bytes_accessed=8 * 2**20, transcendentals=0
        ),
        name="weight_product",
    )(core.reshape(1), acts, own, other)


def widen_kernel(in_ref, out_ref):
    out_ref[...] = in_ref[...].astype(out_ref.dtype)


def widen(array):
    rows, width = array.shape
    block = pl.BlockSpec((rows // 2, width), lambda i: (i, 0))
    return pl.pallas_call(
        widen_kernel,
        grid=(2,),
        in_specs=[block],
        out_specs=block,
        out_shape=jax.ShapeDtypeStruct(array.shape, jnp.float32),
        cost_estimate=pl.CostEstimate(flops=6 * 10**10, bytes_accessed=2**22, transcendentals=0),
        name="widen",
    )(array)


def input_kernel(own_ref, other_ref, weight_ref, _, out_ref):
    blocks, ff, width = weight_ref.shape

    def product(rows_ref):
        total = jnp.zeros((rows_ref.shape[0], ff), jnp.float32)
        for i in range(blocks):
            total += lax.dot_general(
                rows_ref[:, i * width : (i + 1) * width],
                weight_ref[i],
                (((1,), (1,)), ((), ())),
                preferred_element_type=jnp.float32,
            )
        out_ref[...] = total.astype(out_ref.dtype).reshape(out_ref.shape)

    @pl.when(pl.program_id(0) == 0)
    def _():
        product(own_ref)

    @pl.when(pl.program_id(0) == 1)
    def _():
        product(other_ref)


def input_product(own, other, weights, after, quarter):
    tokens, wide = own.shape
    ff = weights.shape[1]
    steps = 2
    rows = tokens // steps
    return pl.pallas_call(
        input_kernel,
        grid=(2, steps),
        in_specs=[
            pl.BlockSpec((rows, wide), lambda h, i: (jnp.where(h == 0, i, steps - 1), 0)),
            pl.BlockSpec((rows, wide), lambda h, i: (jnp.where(h == 0, 0, i), 0)),
            pl.BlockSpec(weights.shape, lambda h, i: (0, 0, 0)),
            pl.BlockSpec(memory_space=pl.ANY),
        ],
        out_specs=pl.BlockSpec((rows // quarter, 1, quarter, ff), lambda h, i: (i, h, 0, 0)),
        out_shape=jax.ShapeDtypeStruct((tokens // quarter, 2, quarter, ff), jnp.bfloat16),
        compiler_params=pltpu.CompilerParams(vmem_limit_bytes=14 * 2**20),
        cost_estimate=pl.CostEstimate(
            flops=4 * ff * tokens * wide, bytes_accessed=8 * 2**20, transcendentals=0
        ),
        name="input_product",
    )(own, other, weights, after)


def on_device(grad_out, signs, weight, activations, outliers):
    n_y, n_zh, n_x, n_zl = (lax.axis_size(a) for a in ("y", "zh", "x", "zl"))
    hidden = n_x * n_zl
    tok, width = grad_out.shape
    ff = activations.shape[1]
    quarter = tok // n_x
    wide = n_x * width
    factor = 1.0 / math.sqrt(width * hidden)
    token_scale = 1.0 / math.sqrt(tok * n_y * n_zh * 2)
    y, zh, core, x = (lax.axis_index(a) for a in ("y", "zh", "c", "x"))

    gathered = lax.all_gather(weight, "x", axis=0)

    channel = ((y * n_zh + zh) * 2 + core) * ff + jnp.arange(ff, dtype=jnp.int32)
    special = jnp.any(channel[:, None] == outliers[None, :], axis=1)
    clipped = jnp.where(special[None, :], activations, jnp.clip(activations, -3.0, 3.0))
    acts = exchanged(clipped.reshape(2, n_x, quarter, ff).transpose(1, 0, 2, 3), "x")

    flips = (2 * signs - 1).astype(jnp.bfloat16)
    signed = grad_out * flips[None, :]
    spread = jnp.broadcast_to(
        signed.reshape(n_x, 1, quarter, width), (n_x, n_zl, quarter, width)
    ).reshape(hidden * quarter, width)
    rows = lax.all_to_all(spread, ("x", "zl"), split_axis=0, concat_axis=0, tiled=True)
    mine = (rotate_rows(rows, width, n_x, n_zl) * factor).astype(jnp.bfloat16)
    mine, acts = lax.optimization_barrier((mine, acts))
    acts = lax.all_gather(acts, "zl", axis=0)

    own = jnp.zeros((n_y, n_zh, quarter, wide), jnp.bfloat16)
    own = lax.dynamic_update_slice(own, spread_over(mine, "y")[:, None], (0, zh, 0, 0))
    along = lax.all_gather(mine, "zh", axis=0)
    along, own, gathered = lax.optimization_barrier((along, own, gathered))
    one, two, three = (picked(along, (zh + r) % n_zh) for r in range(1, n_zh))
    half = quarter // 2
    left = spread_over(jnp.concatenate([two[half:], three], axis=0), "y")
    right = lax.all_gather(jnp.concatenate([one, two[:half]], axis=0), "y", axis=0)
    for block, r, low in (
        (right[:, :quarter], 1, 0),
        (right[:, quarter:], 2, 0),
        (left[:, :half], 2, half),
        (left[:, half:], 3, 0),
    ):
        own = lax.dynamic_update_slice(own, block[:, None], (0, (zh + r) % n_zh, low, 0))
    own = own.reshape(hidden * quarter, wide)
    own, acts = lax.optimization_barrier((own, acts))
    other = lax.ppermute(own, "c", [(0, 1), (1, 0)])

    parts = weight_product(core, acts, own, other, width, token_scale)
    weight_grad = widen(lax.psum_scatter(parts, "x", scatter_dimension=0))

    part = input_product(own, other, gathered, parts, quarter)
    part = lax.all_to_all(part, ("x", "zl"), split_axis=0, concat_axis=0, tiled=True)
    part, weight_grad = lax.optimization_barrier((part, weight_grad))
    part = part.reshape(n_x, n_zl, 2, quarter, ff).astype(jnp.float32)
    summed = jnp.sum(part, axis=1)
    first = jnp.where(core == 0, summed[:, 0], summed[:, 1])
    second = jnp.where(core == 0, summed[:, 1], summed[:, 0])
    summed = jnp.stack([first, second], axis=0).reshape(activations.shape)
    kept = special[None, :] | (jnp.abs(activations.astype(jnp.float32)) <= 3.0)
    input_grad = jnp.where(kept, summed, 0.0).astype(jnp.bfloat16)
    return (input_grad, weight_grad)


def solution(mesh):
    fine = Mesh(mesh.devices.reshape(4, 4, 2, 4, 4), ("y", "zh", "c", "x", "zl"))
    dp, hidden = ("y", "zh", "c"), ("x", "zl")
    in_specs = (P(dp, hidden), P(hidden), P(dp, hidden), P(hidden, dp), P())
    out_specs = (P(hidden, dp), P(dp, hidden))
    return jax.shard_map(
        on_device, mesh=fine, in_specs=in_specs, out_specs=out_specs, check_vma=False
    )
```

time: 257 us -> 170 us (0.66)
  waiting for transfers between devices: 131 us -> 44.1 us
  starting transfers between devices: 79.8 us -> 46.8 us
  blocking collectives: 8.58 us -> 38.2 us
  matrix products: 11.7 us -> 1.46 us
  Pallas kernels: 0 us -> 10.1 us
  local copies, waits for them, and re-layouts: 2.95 us -> 11.7 us
  other arithmetic: 7.61 us -> 3.08 us
    ppermute x15 -> x3, starting transfers between devices: 55.6 us -> 10.6 us  [shifted(): return lax.ppermute(array, axis, [(i, (i + by) % n) for i in range(n)])]
    all_gather x0 -> x2, blocking collectives: none -> 38.2 us  [the longest x1 25.9 us: on_device(): along = lax.all_gather(mine, 'zh', axis=0)]
    all_gather x2, waiting for transfers between devices: 31.9 us -> 0.99 us  [the longest x1 0.97 us: on_device(): acts = lax.all_gather(acts, 'zl', axis=0)]
    all_to_all x1 -> x3, waiting for transfers between devices: 26.7 us -> 6.27 us  [the longest x2 6.27 us: spread_over(): return lax.all_to_all(copies, axis, split_axis=0, concat_axis=0, tiled=True)]
    ppermute x15 -> x3, waiting for transfers between devices: 19.4 us -> 1.99 us  [shifted(): return lax.ppermute(array, axis, [(i, (i + by) % n) for i in range(n)])]
    all_to_all x1, waiting for transfers between devices: 14.8 us -> 2.56 us  [on_device(): lax.all_to_all(spread, ('x', 'zl'), split_axis=0, concat_axis=0, tiled=True)]
    all_to_all x1 -> x3, starting transfers between devices: 3.79 us -> 15.6 us  [the longest x2 7.96 us: spread_over(): return lax.all_to_all(copies, axis, split_axis=0, concat_axis=0, tiled=True)]
    dot_general x4 -> x0, matrix products: 10.2 us -> none  [product(): lax.dot_general(a, b, (dims, ((), ())), preferred_element_type=jnp.float32)]
  transfers between devices with their start and end apart: 21 -> 11, of which waited for: 11 -> 6; matrix products, arithmetic and copies ran while one was open for 2% -> 6% of each run, Pallas kernels for 0% -> 3%
where the time goes in v3:
time: 170 us; the launch traced here: 169 us
  starting transfers between devices  46.8 us (28%)
  waiting for transfers between devices  44.1 us (26%)
  blocking collectives  38.2 us (22%)
  between operations  14.1 us (8%)
  local copies, waits for them, and re-layouts  11.7 us (7%)
  Pallas kernels  10.1 us (6%)
  other arithmetic  3.08 us (2%)
    reduce_scatter x1, waiting for transfers between devices, on_device(): weight_grad = widen(lax.psum_scatter(parts, 'x', scatter_dimension=0))  27.8 us
    all_gather x1, blocking collectives, on_device(): along = lax.all_gather(mine, 'zh', axis=0)  25.9 us
    all_gather x1, blocking collectives, on_device(): lax.all_gather(jnp.concatenate([one, two[:half]], axis=0), 'y', axis=0)  12.2 us
    ppermute x1, starting transfers between devices, on_device(): other = lax.ppermute(own, 'c', [(0, 1), (1, 0)])  11.5 us
    ppermute x3, starting transfers between devices, shifted(): return lax.ppermute(array, axis, [(i, (i + by) % n) for i in range(n)])  10.6 us
    all_to_all x1, starting transfers between devices, on_device(): lax.all_to_all(spread, ('x', 'zl'), split_axis=0, concat_axis=0, tiled=True)  9.01 us
    all_to_all x2, starting transfers between devices, spread_over(): return lax.all_to_all(copies, axis, split_axis=0, concat_axis=0, tiled=True)  7.96 us
    all_to_all x1, starting transfers between devices, on_device(): lax.all_to_all(part, ('x', 'zl'), split_axis=0, concat_axis=0, tiled=True)  7.64 us
  transfers between devices with their start and end apart: 11, of which 6 were waited for; matrix products, arithmetic and copies ran while one was open for 6% of the time, Pallas kernels for 3%

profile of v3, /device:TPU:1, one launch (start us, length us, event | category | flops | bytes accessed | tf_op | source)
XLA Modules:
  0.0 169.4 jit_solution(16527636832449070470)
XLA Ops:
  8.6 0.9 broadcast_multiply_fusion
  9.5 0.8 broadcast_in_dim.44
  10.4 9.0 %all-to-all-start = ((bf16[16,32,512]{2,1,0:T(8,128)(2,1)}), bf16[16,32,512]{2,1,0:T(8,128)(2,1)S(1)}, u32[]{:S(2)}, u32[]{:S(2)}) async-start(bf16[16,32,512]{2,1,0:T(8,128)(2,1)} %bitcast.1), calls=%async_computation | async-start | bytes 1048576 | tf_op jit(solution)/shard_map/all_to_all | solution.py:200
  19.8 3.2 %collective-permute-start = (bf16[2,32,512]{2,1,0:T(8,128)(2,1)S(1)}, bf16[2,32,512]{2,1,0:T(8,128)(2,1)S(1)}, u32[]{:S(2)}, u32[]{:S(2)}) collective-permute-start(bf16[2,32,512]{2,1,0:T(8,128)(2,1)S(1)} %get-tuple-element.26), channel_id=1, source_target_pairs={{0,4},{4,8},{8,12},{12,0},{1,5},{5,9},{9,13},{13,1},{2,6},{6,10},{... | collective-permute-start | bytes 196616 | tf_op jit(solution)/shard_map/ppermute | solution.py:42
  23.0 4.3 %collective-permute-start.1 = (bf16[2,32,512]{2,1,0:T(8,128)(2,1)S(1)}, bf16[2,32,512]{2,1,0:T(8,128)(2,1)S(1)}, u32[]{:S(2)}, u32[]{:S(2)}) collective-permute-start(bf16[2,32,512]{2,1,0:T(8,128)(2,1)S(1)} %get-tuple-element.25), channel_id=1, source_target_pairs={{0,8},{4,12},{8,0},{12,4},{1,9},{5,13},{9,1},{13,5},{2,10},{6,14},... | collective-permute-start | bytes 196616 | tf_op jit(solution)/shard_map/ppermute | solution.py:42
  27.3 3.1 %collective-permute-start.2 = (bf16[2,32,512]{2,1,0:T(8,128)(2,1)S(1)}, bf16[2,32,512]{2,1,0:T(8,128)(2,1)S(1)}, u32[]{:S(2)}, u32[]{:S(2)}) collective-permute-start(bf16[2,32,512]{2,1,0:T(8,128)(2,1)S(1)} %get-tuple-element.24), channel_id=1, source_target_pairs={{0,12},{4,0},{8,4},{12,8},{1,13},{5,1},{9,5},{13,9},{2,14},{6,2},{... | collective-permute-start | bytes 196616 | tf_op jit(solution)/shard_map/ppermute | solution.py:42
  30.5 2.0 %collective-permute-done.2 = bf16[2,32,512]{2,1,0:T(8,128)(2,1)S(1)} collective-permute-done((bf16[2,32,512]{2,1,0:T(8,128)(2,1)S(1)}, bf16[2,32,512]{2,1,0:T(8,128)(2,1)S(1)}, u32[]{:S(2)}, u32[]{:S(2)}) %collective-permute-start.2) | collective-permute-done | bytes 65568 | tf_op jit(solution)/shard_map/ppermute | solution.py:42
  32.5 2.6 %all-to-all-done = bf16[16,32,512]{2,1,0:T(8,128)(2,1)S(1)} async-done(((bf16[16,32,512]{2,1,0:T(8,128)(2,1)}), bf16[16,32,512]{2,1,0:T(8,128)(2,1)S(1)}, u32[]{:S(2)}, u32[]{:S(2)}) %all-to-all-start) | async-done | bytes 524320 | tf_op jit(solution)/shard_map/all_to_all | solution.py:200
  35.1 1.5 fusion
  36.6 0.8 broadcast_in_dim.51
  37.5 4.2 %all-to-all-start.1 = ((bf16[4,32,2048]{2,1,0:T(8,128)(2,1)}), bf16[4,32,2048]{2,1,0:T(8,128)(2,1)S(1)}, u32[]{:S(2)}, u32[]{:S(2)}) async-start(bf16[4,32,2048]{2,1,0:T(8,128)(2,1)} %broadcast_in_dim.51), calls=%async_computation.1 | async-start | bytes 1048576 | tf_op jit(solution)/shard_map/all_to_all | solution.py:62
  41.7 0.7 copy.25
  42.4 25.9 %all-gather = bf16[128,2048]{1,0:T(8,128)(2,1)S(1)} all-gather(bf16[32,2048]{1,0:T(8,128)(2,1)S(1)} %fusion.34), channel_id=2, replica_groups=mesh['y'=4,'zh'=4,'c'=2,'x'=4,'zl'=4] {'zh'}, dimensions={0}, use_global_device_ids=true | all-gather | bytes 655360 | tf_op jit(solution)/shard_map/all_gather | solution.py:207
  68.8 12.2 %all-gather.2 = bf16[192,2048]{1,0:T(8,128)(2,1)} all-gather(bf16[48,2048]{1,0:T(8,128)(2,1)S(1)} %pad_maximum_fusion.1), channel_id=4, replica_groups=mesh['y'=4,'zh'=4,'c'=2,'x'=4,'zl'=4] {'y'}, dimensions={0}, use_global_device_ids=true | all-gather | bytes 983040 | tf_op jit(solution)/shard_map/all_gather | solution.py:212
  81.1 1.0 broadcast_in_dim.100
  82.0 3.8 %all-to-all-start.2 = ((bf16[4,48,2048]{2,1,0:T(8,128)(2,1)}), bf16[4,48,2048]{2,1,0:T(8,128)(2,1)S(1)}, u32[]{:S(2)}, u32[]{:S(2)}) async-start(bf16[4,48,2048]{2,1,0:T(8,128)(2,1)} %broadcast_in_dim.100), calls=%async_computation.2 | async-start | bytes 1572864 | tf_op jit(solution)/shard_map/all_to_all | solution.py:62
  85.8 1.1 fusion.6
  86.9 1.0 fusion.33
  87.9 6.3 %all-to-all-done.2 = bf16[4,48,2048]{2,1,0:T(8,128)(2,1)S(1)} async-done(((bf16[4,48,2048]{2,1,0:T(8,128)(2,1)}), bf16[4,48,2048]{2,1,0:T(8,128)(2,1)S(1)}, u32[]{:S(2)}, u32[]{:S(2)}) %all-to-all-start.2) | async-done | bytes 786464 | tf_op jit(solution)/shard_map/all_to_all | solution.py:62
  94.2 1.0 all-gather.9.cloned.1.call-done
  95.2 11.5 %collective-permute-start.3 = (bf16[512,2048]{1,0:T(8,128)(2,1)S(1)}, bf16[512,2048]{1,0:T(8,128)(2,1)S(1)}, u32[]{:S(2)}, u32[]{:S(2)}) collective-permute-start(bf16[512,2048]{1,0:T(8,128)(2,1)S(1)} %bitcast.90), channel_id=1, source_target_pairs={{0,16},{16,0},{1,17},{17,1},{2,18},{18,2},{3,19},{19,3},{4,20},{20... | collective-permute-start | bytes 6291464 | tf_op jit(solution)/shard_map/ppermute | solution.py:222
  106.7 3.8 %collective-permute-done.3.refs_3_.other_ref = bf16[512,2048]{1,0:T(8,128)(2,1)S(1)} collective-permute-done((bf16[512,2048]{1,0:T(8,128)(2,1)S(1)}, bf16[512,2048]{1,0:T(8,128)(2,1)S(1)}, u32[]{:S(2)}, u32[]{:S(2)}) %collective-permute-start.3) | collective-permute-done | bytes 2097184 | tf_op jit(solution)/shard_map/ppermute | solution.py:222
  110.5 1.2 copy-done.3
  111.7 4.4 %weight_product.1._ = bf16[4,512,512]{2,1,0:T(8,128)(2,1)} custom-call(s32[1]{0:T(128)} %bitcast.33.refs_0_, bf16[4,4,2,32,512]{4,3,2,1,0:T(8,128)(2,1)S(1)} %bitcast.94, bf16[512,2048]{1,0:T(8,128)(2,1)S(1)} %bitcast.91, bf16[512,2048]{1,0:T(8,128)(2,1)S(1)} %collective-permute-done.3.refs_3_.other_ref), custom_call_target="tpu_custom_call" | custom-call | flops 2147483648 | bytes 8388608 | tf_op jit(solution)/shard_map/weight_product/pallas_call | solution.py:89
  116.1 1.3 copy-done.1
  117.5 1.6 copy-done
  119.0 1.6 copy-done.2
  120.6 3.8 %input_product.1 = bf16[16,2,32,512]{3,2,1,0:T(8,128)(2,1)} custom-call(bf16[512,2048]{1,0:T(8,128)(2,1)S(1)} %bitcast.92, bf16[512,2048]{1,0:T(8,128)(2,1)S(1)} %copy-done.2, bf16[4,512,512]{2,1,0:T(8,128)(2,1)S(1)} %bitcast.93, bf16[4,512,512]{2,1,0:T(8,128)(2,1)} %weight_product.1._), custom_call_target="tpu_custom_call" | custom-call | flops 2147483648 | bytes 8388608 | tf_op jit(solution)/shard_map/input_product/pallas_call | solution.py:158
  124.4 7.6 %all-to-all-start.3 = ((bf16[16,2,32,512]{3,2,1,0:T(8,128)(2,1)}), bf16[16,2,32,512]{3,2,1,0:T(8,128)(2,1)S(1)}, u32[]{:S(2)}, u32[]{:S(2)}) async-start(bf16[16,2,32,512]{3,2,1,0:T(8,128)(2,1)} %input_product.1), calls=%async_computation.3 | async-start | bytes 2097152 | tf_op jit(solution)/shard_map/all_to_all | solution.py:228
  132.0 27.8 %reduce-scatter.2.cloned.1.call-done = bf16[1,512,512]{2,1,0:T(8,128)(2,1)} async-done(((bf16[4,512,512]{2,1,0:T(8,128)(2,1)}), bf16[1,512,512]{2,1,0:T(8,128)(2,1)}) %reduce-scatter.2.cloned.1.call-update) | async-done | bytes 524304 | tf_op jit(solution)/shard_map/reduce_scatter | solution.py:225
  159.8 2.0 %widen.1 = f32[512,512]{1,0:T(8,128)} custom-call(bf16[512,512]{1,0:T(8,128)(2,1)} %bitcast.103), custom_call_target="tpu_custom_call" | custom-call | flops 60000002048 | bytes 4194304 | tf_op jit(solution)/shard_map/widen/pallas_call | solution.py:119
  162.0 0.9 fusion.7
  (47 shorter events, 2.6 us)
Async XLA Ops:
  7.2 12.3 %copy-start.5 = (s32[128]{0:T(128)S(1)}, s32[128]{0:T(128)}, u32[]{:S(2)}) copy-start(s32[128]{0:T(128)} %param.9) | copy-start | bytes 1540
  7.2 12.5 %copy-start.4 = (bf16[256,512]{1,0:T(8,128)(2,1)S(1)}, bf16[256,512]{1,0:T(8,128)(2,1)}, u32[]{:S(2)}) copy-start(bf16[256,512]{1,0:T(8,128)(2,1)} %param.8) | copy-start | bytes 786436
  7.2 61.5 %all-gather.7.cloned.1.call-start = ((), (), s32[]{:S(2)}) async-start(), calls=%async_computation.6 | async-start | bytes 2621440 | tf_op jit(solution)/shard_map/all_gather | solution.py:188
  10.4 24.7 %all-to-all-start = ((bf16[16,32,512]{2,1,0:T(8,128)(2,1)}), bf16[16,32,512]{2,1,0:T(8,128)(2,1)S(1)}, u32[]{:S(2)}, u32[]{:S(2)}) async-start(bf16[16,32,512]{2,1,0:T(8,128)(2,1)} %bitcast.1), calls=%async_computation | async-start | bytes 1048576 | tf_op jit(solution)/shard_map/all_to_all | solution.py:200
  19.8 10.7 %collective-permute-start = (bf16[2,32,512]{2,1,0:T(8,128)(2,1)S(1)}, bf16[2,32,512]{2,1,0:T(8,128)(2,1)S(1)}, u32[]{:S(2)}, u32[]{:S(2)}) collective-permute-start(bf16[2,32,512]{2,1,0:T(8,128)(2,1)S(1)} %get-tuple-element.26), channel_id=1, source_target_pairs={{0,4},{4,8},{8,12},{12,0},{1,5},{5,9},{9,13},{13,1},{2,6},{6,10},{... | collective-permute-start | bytes 196616 | tf_op jit(solution)/shard_map/ppermute | solution.py:42
  23.0 7.5 %collective-permute-start.1 = (bf16[2,32,512]{2,1,0:T(8,128)(2,1)S(1)}, bf16[2,32,512]{2,1,0:T(8,128)(2,1)S(1)}, u32[]{:S(2)}, u32[]{:S(2)}) collective-permute-start(bf16[2,32,512]{2,1,0:T(8,128)(2,1)S(1)} %get-tuple-element.25), channel_id=1, source_target_pairs={{0,8},{4,12},{8,0},{12,4},{1,9},{5,13},{9,1},{13,5},{2,10},{6,14},... | collective-permute-start | bytes 196616 | tf_op jit(solution)/shard_map/ppermute | solution.py:42
  27.3 5.2 %collective-permute-start.2 = (bf16[2,32,512]{2,1,0:T(8,128)(2,1)S(1)}, bf16[2,32,512]{2,1,0:T(8,128)(2,1)S(1)}, u32[]{:S(2)}, u32[]{:S(2)}) collective-permute-start(bf16[2,32,512]{2,1,0:T(8,128)(2,1)S(1)} %get-tuple-element.24), channel_id=1, source_target_pairs={{0,12},{4,0},{8,4},{12,8},{1,13},{5,1},{9,5},{13,9},{2,14},{6,2},{... | collective-permute-start | bytes 196616 | tf_op jit(solution)/shard_map/ppermute | solution.py:42
  37.5 30.9 %all-to-all-start.1 = ((bf16[4,32,2048]{2,1,0:T(8,128)(2,1)}), bf16[4,32,2048]{2,1,0:T(8,128)(2,1)S(1)}, u32[]{:S(2)}, u32[]{:S(2)}) async-start(bf16[4,32,2048]{2,1,0:T(8,128)(2,1)} %broadcast_in_dim.51), calls=%async_computation.1 | async-start | bytes 1048576 | tf_op jit(solution)/shard_map/all_to_all | solution.py:62
  41.7 53.5 %all-gather.9.cloned.1.call-start = ((), (), s32[]{:S(2)}) async-start(), calls=%async_computation.7 | async-start | bytes 1310720 | tf_op jit(solution)/shard_map/all_gather | solution.py:203
  82.0 12.1 %all-to-all-start.2 = ((bf16[4,48,2048]{2,1,0:T(8,128)(2,1)}), bf16[4,48,2048]{2,1,0:T(8,128)(2,1)S(1)}, u32[]{:S(2)}, u32[]{:S(2)}) async-start(bf16[4,48,2048]{2,1,0:T(8,128)(2,1)} %broadcast_in_dim.100), calls=%async_computation.2 | async-start | bytes 1572864 | tf_op jit(solution)/shard_map/all_to_all | solution.py:62
  85.8 74.0 %reduce-scatter.2.cloned.1.call-start = ((), (), s32[]{:S(2)}) async-start(), calls=%async_computation.5 | async-start | bytes 2621440 | tf_op jit(solution)/shard_map/reduce_scatter | solution.py:225
  95.2 15.3 %collective-permute-start.3 = (bf16[512,2048]{1,0:T(8,128)(2,1)S(1)}, bf16[512,2048]{1,0:T(8,128)(2,1)S(1)}, u32[]{:S(2)}, u32[]{:S(2)}) collective-permute-start(bf16[512,2048]{1,0:T(8,128)(2,1)S(1)} %bitcast.90), channel_id=1, source_target_pairs={{0,16},{16,0},{1,17},{17,1},{2,18},{18,2},{3,19},{19,3},{4,20},{20... | collective-permute-start | bytes 6291464 | tf_op jit(solution)/shard_map/ppermute | solution.py:222
  110.5 1.2 copy-start.3
  116.1 1.3 copy-start.1
  117.4 1.6 copy-start
  119.0 1.6 copy-start.2
  124.4 37.4 %all-to-all-start.3 = ((bf16[16,2,32,512]{3,2,1,0:T(8,128)(2,1)}), bf16[16,2,32,512]{3,2,1,0:T(8,128)(2,1)S(1)}, u32[]{:S(2)}, u32[]{:S(2)}) async-start(bf16[16,2,32,512]{3,2,1,0:T(8,128)(2,1)} %input_product.1), calls=%async_computation.3 | async-start | bytes 2097152 | tf_op jit(solution)/shard_map/all_to_all | solution.py:228
Sparse Core Ops, SparseCore 0:
  10.1 43.7 all-gather.6
  56.6 38.5 all-gather.8
  117.6 42.2 reduce-scatter.1

commit v4 on v3

v4 whole, which is shorter than its diff:
```python
import math

import jax
import jax.numpy as jnp
from jax import lax
from jax.experimental import pallas as pl
from jax.experimental.pallas import tpu as pltpu
from jax.sharding import Mesh, PartitionSpec as P


def hadamard_table(order):
    index = jnp.arange(order, dtype=jnp.int32)
    count = jnp.zeros((order, order), jnp.int32)
    for level in range(order.bit_length() - 1):
        step = 2**level
        count = count + index[:, None] // step % 2 * (index[None, :] // step % 2)
    return jnp.where(count % 2 == 0, 1.0, -1.0).astype(jnp.float32)


def parity_signs(a, b):
    both = jnp.bitwise_and(a, b)
    return (1 - 2 * (jnp.bitwise_xor(both, both >> 1) & 1)).astype(jnp.float32)


def rotate_rows(rows, width, n_x, n_zl):
    tokens = rows.shape[0] // (n_x * n_zl)
    local = jnp.dot(
        rows, hadamard_table(width).astype(jnp.bfloat16), preferred_element_type=jnp.float32
    )
    local = local.reshape(n_x, n_zl, tokens, width)
    every = jnp.arange(n_zl, dtype=jnp.int32)
    local = jnp.sum(
        local * parity_signs(lax.axis_index("zl"), every)[None, :, None, None], axis=1
    )
    b0, b1, b2, b3 = (local[i] for i in range(n_x))
    s0, d0, s1, d1 = b0 + b1, b0 - b1, b2 + b3, b2 - b3
    return jnp.concatenate([s0 + s1, d0 + d1, s0 - s1, d0 - d1], axis=1)


def signed_kernel(signs_ref, rows_ref, out_ref):
    n_x, n_zl, quarter, _ = out_ref.shape
    flips = (2 * signs_ref[...] - 1).astype(rows_ref.dtype)
    for i in range(n_x):
        rows = rows_ref[i * quarter : (i + 1) * quarter, :] * flips
        for j in range(n_zl):
            out_ref[i, j] = rows


def signed_rows(grad_out, signs, n_x, n_zl):
    tok, width = grad_out.shape
    whole = pl.BlockSpec(memory_space=pltpu.VMEM)
    return pl.pallas_call(
        signed_kernel,
        in_specs=[whole, whole],
        out_specs=whole,
        out_shape=jax.ShapeDtypeStruct((n_x, n_zl, tok // n_x, width), grad_out.dtype),
        cost_estimate=pl.CostEstimate(flops=0, bytes_accessed=2**20, transcendentals=0),
        name="signed_rows",
    )(signs[None, :], grad_out)


def repeat_kernel(rows_ref, out_ref):
    for i in range(out_ref.shape[0]):
        out_ref[i] = rows_ref[...]


def repeated(rows, times):
    whole = pl.BlockSpec(memory_space=pltpu.VMEM)
    return pl.pallas_call(
        repeat_kernel,
        in_specs=[whole],
        out_specs=whole,
        out_shape=jax.ShapeDtypeStruct((times,) + rows.shape, rows.dtype),
        compiler_params=pltpu.CompilerParams(vmem_limit_bytes=16 * 2**20),
        cost_estimate=pl.CostEstimate(flops=0, bytes_accessed=2**21, transcendentals=0),
        name="repeated",
    )(rows)


def shifted(array, axis, by):
    n = lax.axis_size(axis)
    return lax.ppermute(array, axis, [(i, (i + by) % n) for i in range(n)])


def picked(array, index):
    return lax.dynamic_index_in_dim(array, index, 0, keepdims=False)


def exchanged(pieces, axis):
    n = lax.axis_size(axis)
    me = lax.axis_index(axis)
    came = pieces
    for by in range(1, n):
        piece = shifted(picked(pieces, (me + by) % n), axis, by)
        came = lax.dynamic_update_slice_in_dim(came, piece[None], (me + n - by) % n, 0)
    return came


def spread_over(array, axis):
    n = lax.axis_size(axis)
    copies = repeated(array, n)
    return lax.all_to_all(copies, axis, split_axis=0, concat_axis=0, tiled=True)


def turn_kernel(core_ref, acts_ref, out_ref, rows_ref):
    n_zl, n_x, _, quarter, _ = acts_ref.shape
    tokens = n_zl * n_x * quarter
    for half in range(2):
        core = jnp.bitwise_xor(core_ref[0], half)
        for i in range(n_x):
            for j in range(n_zl):
                at = half * tokens + (i * n_zl + j) * quarter
                rows_ref[at : at + quarter, :] = acts_ref[j, i, core]
    out_ref[...] = rows_ref[...].T


def turned(core, acts):
    ff = acts.shape[-1]
    tokens = acts.size // ff
    return pl.pallas_call(
        turn_kernel,
        in_specs=[
            pl.BlockSpec(memory_space=pltpu.SMEM),
            pl.BlockSpec(memory_space=pltpu.VMEM),
        ],
        out_specs=pl.BlockSpec(memory_space=pltpu.VMEM),
        out_shape=jax.ShapeDtypeStruct((ff, tokens), acts.dtype),
        scratch_shapes=[pltpu.VMEM((tokens, ff), acts.dtype)],
        compiler_params=pltpu.CompilerParams(vmem_limit_bytes=16 * 2**20),
        cost_estimate=pl.CostEstimate(flops=6 * 10**10, bytes_accessed=2**21, transcendentals=0),
        name="turned",
    )(core.reshape(1), acts)


def input_part(half, rows_ref, weight_refs, part_ref, out_ref, sends):
    ff, width = weight_refs[0].shape
    groups, quarter, _ = part_ref.shape
    steps = 2
    rows = rows_ref.shape[0] // steps
    out = []
    for j in range(steps):
        total = jnp.zeros((rows, ff), jnp.float32)
        for i, weight_ref in enumerate(weight_refs):
            total += lax.dot_general(
                rows_ref[j * rows : (j + 1) * rows, i * width : (i + 1) * width],
                weight_ref[...],
                (((1,), (1,)), ((), ())),
                preferred_element_type=jnp.float32,
            )
        at = pl.ds(j * (groups // steps), groups // steps)
        part_ref[at] = total.astype(part_ref.dtype).reshape(groups // steps, quarter, ff)
        out.append(pltpu.make_async_copy(part_ref.at[at], out_ref.at[at, half], sends.at[j]))
        out[-1].start()
    return out


def own_kernel(
    acts_ref, rows_ref, weight_ref, weight_part_ref, input_ref, _, held_ref, part_ref, fetches, sends
):
    blocks, _, width = weight_part_ref.shape
    tokens = rows_ref.shape[0]
    fetch = [
        pltpu.make_async_copy(weight_ref.at[i], held_ref.at[i], fetches.at[i])
        for i in range(blocks)
    ]
    for copy in fetch:
        copy.start()
    for i in range(blocks):
        weight_part_ref[i] = jnp.dot(
            acts_ref[:, :tokens],
            rows_ref[:, i * width : (i + 1) * width],
            preferred_element_type=jnp.float32,
        )
    for copy in fetch:
        copy.wait()
    held = [held_ref.at[i] for i in range(blocks)]
    for copy in input_part(0, rows_ref, held, part_ref, input_ref, sends):
        copy.wait()


def other_kernel(
    scale, acts_ref, rows_ref, weight_ref, own_ref, _, __, input_ref, out_ref,
    held_ref, part_ref, weight_part_ref, fetches, sends, weight_sends
):
    blocks, _, width = own_ref.shape
    tokens = rows_ref.shape[0]
    fetch = [
        pltpu.make_async_copy(weight_ref.at[i], held_ref.at[i], fetches.at[i])
        for i in range(blocks)
    ]
    for copy in fetch:
        copy.start()
    out = []
    for i in range(blocks):
        part = own_ref[i] + jnp.dot(
            acts_ref[:, tokens:],
            rows_ref[:, i * width : (i + 1) * width],
            preferred_element_type=jnp.float32,
        )
        weight_part_ref[i] = (part * scale).astype(weight_part_ref.dtype)
        out.append(
            pltpu.make_async_copy(weight_part_ref.at[i], out_ref.at[i], weight_sends.at[i])
        )
        out[-1].start()
    for copy in fetch:
        copy.wait()
    held = [held_ref.at[i] for i in range(blocks)]
    out += input_part(1, rows_ref, held, part_ref, input_ref, sends)
    for copy in out:
        copy.wait()


def products(acts, own, other, weights, quarter, scale):
    blocks, ff, width = weights.shape
    tokens, wide = own.shape
    groups = tokens // quarter
    whole = pl.BlockSpec(memory_space=pltpu.VMEM)
    hbm = pl.BlockSpec(memory_space=pltpu.HBM)
    estimate = pl.CostEstimate(
        flops=4 * ff * tokens * wide, bytes_accessed=8 * 2**20, transcendentals=0
    )
    params = pltpu.CompilerParams(vmem_limit_bytes=20 * 2**20)
    input_shape = jax.ShapeDtypeStruct((groups, 2, quarter, ff), jnp.bfloat16)
    weight_shape = jax.ShapeDtypeStruct(weights.shape, jnp.bfloat16)
    scratch = [
        pltpu.VMEM(weights.shape, weights.dtype),
        pltpu.VMEM((groups, quarter, ff), jnp.bfloat16),
    ]
    sems = [pltpu.SemaphoreType.DMA((blocks,)), pltpu.SemaphoreType.DMA((2,))]
    first, input_part, weight_part = pl.pallas_call(
        own_kernel,
        in_specs=[whole, whole, hbm],
        out_specs=[whole, hbm, hbm],
        out_shape=[
            jax.ShapeDtypeStruct(weights.shape, jnp.float32),
            input_shape,
            weight_shape,
        ],
        scratch_shapes=scratch + sems,
        compiler_params=params,
        cost_estimate=estimate,
        name="products_own",
    )(acts, own, weights)
    input_part, weight_part = pl.pallas_call(
        lambda *refs: other_kernel(scale, *refs),
        in_specs=[whole, whole, hbm, whole, hbm, hbm],
        out_specs=[hbm, hbm],
        out_shape=[input_shape, weight_shape],
        input_output_aliases={4: 0, 5: 1},
        scratch_shapes=scratch
        + [pltpu.VMEM(weights.shape, jnp.bfloat16)]
        + sems
        + [pltpu.SemaphoreType.DMA((blocks,))],
        compiler_params=params,
        cost_estimate=estimate,
        name="products_other",
    )(acts, other, weights, first, input_part, weight_part)
    return weight_part, input_part


def widen_kernel(in_ref, out_ref):
    out_ref[...] = in_ref[...].astype(out_ref.dtype)


def widen(array):
    rows, width = array.shape
    block = pl.BlockSpec((rows // 2, width), lambda i: (i, 0))
    return pl.pallas_call(
        widen_kernel,
        grid=(2,),
        in_specs=[block],
        out_specs=block,
        out_shape=jax.ShapeDtypeStruct(array.shape, jnp.float32),
        cost_estimate=pl.CostEstimate(flops=6 * 10**10, bytes_accessed=2**22, transcendentals=0),
        name="widen",
    )(array)


def on_device(grad_out, signs, weight, activations, outliers):
    n_y, n_zh, n_x, n_zl = (lax.axis_size(a) for a in ("y", "zh", "x", "zl"))
    hidden = n_x * n_zl
    tok, width = grad_out.shape
    ff = activations.shape[1]
    quarter = tok // n_x
    wide = n_x * width
    factor = 1.0 / math.sqrt(width * hidden)
    token_scale = 1.0 / math.sqrt(tok * n_y * n_zh * 2)
    y, zh, core, x = (lax.axis_index(a) for a in ("y", "zh", "c", "x"))

    gathered = lax.all_gather(weight, "x", axis=0)

    channel = ((y * n_zh + zh) * 2 + core) * ff + jnp.arange(ff, dtype=jnp.int32)
    special = jnp.any(channel[:, None] == outliers[None, :], axis=1)
    clipped = jnp.where(special[None, :], activations, jnp.clip(activations, -3.0, 3.0))
    acts = exchanged(clipped.reshape(2, n_x, quarter, ff).transpose(1, 0, 2, 3), "x")

    spread = signed_rows(grad_out, signs, n_x, n_zl).reshape(hidden * quarter, width)
    rows = lax.all_to_all(spread, ("x", "zl"), split_axis=0, concat_axis=0, tiled=True)
    mine = (rotate_rows(rows, width, n_x, n_zl) * factor).astype(jnp.bfloat16)
    mine, acts = lax.optimization_barrier((mine, acts))
    acts = lax.all_gather(acts, "zl", axis=0)

    along = lax.all_gather(mine, "zh", axis=0)
    along, gathered = lax.optimization_barrier((along, gathered))
    own = spread_over(along.reshape(-1, wide), "y").reshape(-1, wide)
    own, acts = lax.optimization_barrier((own, turned(core, acts)))
    other = lax.ppermute(own, "c", [(0, 1), (1, 0)])

    parts, part = products(acts, own, other, gathered, quarter, token_scale)
    weight_grad = widen(lax.psum_scatter(parts, "x", scatter_dimension=0))
    part = lax.all_to_all(part, ("x", "zl"), split_axis=0, concat_axis=0, tiled=True)
    part, weight_grad = lax.optimization_barrier((part, weight_grad))
    part = part.reshape(n_x, n_zl, 2, quarter, ff).astype(jnp.float32)
    summed = jnp.sum(part, axis=1)
    first = jnp.where(core == 0, summed[:, 0], summed[:, 1])
    second = jnp.where(core == 0, summed[:, 1], summed[:, 0])
    summed = jnp.stack([first, second], axis=0).reshape(activations.shape)
    kept = special[None, :] | (jnp.abs(activations.astype(jnp.float32)) <= 3.0)
    input_grad = jnp.where(kept, summed, 0.0).astype(jnp.bfloat16)
    return (input_grad, weight_grad)


def solution(mesh):
    fine = Mesh(mesh.devices.reshape(4, 4, 2, 4, 4), ("y", "zh", "c", "x", "zl"))
    dp, hidden = ("y", "zh", "c"), ("x", "zl")
    in_specs = (P(dp, hidden), P(hidden), P(dp, hidden), P(hidden, dp), P())
    out_specs = (P(hidden, dp), P(dp, hidden))
    return jax.shard_map(
        on_device, mesh=fine, in_specs=in_specs, out_specs=out_specs, check_vma=False
    )
```

time: 170 us -> 160 us (0.941); the launches traced: 169 us -> 157 us
  waiting for transfers between devices: 44.1 us -> 66.5 us
  starting transfers between devices: 46.8 us -> 32.6 us
  blocking collectives: 38.2 us -> 25.3 us
  local copies, waits for them, and re-layouts: 11.7 us -> 3.6 us
  Pallas kernels: 10.1 us -> 12.4 us
    all_gather x1, waiting for transfers between devices: 0.97 us -> 26.8 us  [on_device(): acts = lax.all_gather(acts, 'zl', axis=0)]
    all_gather x1 -> x0, blocking collectives: 12.2 us -> none  [on_device(): lax.all_gather(jnp.concatenate([one, two[:half]], axis=0), 'y', axis=0)]
    ppermute x1, starting transfers between devices: 11.5 us -> 2.8 us  [on_device(): other = lax.ppermute(own, 'c', [(0, 1), (1, 0)])]
    all_to_all x2 -> x1, waiting for transfers between devices: 6.27 us -> 0.01 us  [spread_over(): return lax.all_to_all(copies, axis, split_axis=0, concat_axis=0, tiled=True)]
    reduce_scatter x1, waiting for transfers between devices: 27.8 us -> 33.3 us  [on_device(): weight_grad = widen(lax.psum_scatter(parts, 'x', scatter_dimension=0))]
    ppermute x1, waiting for transfers between devices: 3.76 us -> 0.01 us  [on_device(): other = lax.ppermute(own, 'c', [(0, 1), (1, 0)])]
    all_to_all x2 -> x1, starting transfers between devices: 7.96 us -> 4.94 us  [spread_over(): return lax.all_to_all(copies, axis, split_axis=0, concat_axis=0, tiled=True)]
    unnamed x12 -> x8, local copies, waits for them, and re-layouts: 5.75 us -> 2.82 us
  transfers between devices with their start and end apart: 11 -> 10, of which waited for: 6 -> 4; matrix products, arithmetic and copies ran while one was open for 6% -> 2% of each run, Pallas kernels for 3% -> 6%
where the time goes in v4:
time: 160 us; the launch traced here: 157 us
  waiting for transfers between devices  66.5 us (42%)
  starting transfers between devices  32.6 us (20%)
  blocking collectives  25.3 us (16%)
  between operations  14.1 us (9%)
  Pallas kernels  12.4 us (8%)
  local copies, waits for them, and re-layouts  3.6 us (2%)
    reduce_scatter x1, waiting for transfers between devices, on_device(): weight_grad = widen(lax.psum_scatter(parts, 'x', scatter_dimension=0))  33.3 us
    all_gather x1, waiting for transfers between devices, on_device(): acts = lax.all_gather(acts, 'zl', axis=0)  26.8 us
    all_gather x1, blocking collectives, on_device(): along = lax.all_gather(mine, 'zh', axis=0)  25.3 us
    ppermute x3, starting transfers between devices, shifted(): return lax.ppermute(array, axis, [(i, (i + by) % n) for i in range(n)])  9.45 us
    all_to_all x1, starting transfers between devices, on_device(): lax.all_to_all(spread, ('x', 'zl'), split_axis=0, concat_axis=0, tiled=True)  9.01 us
    all_to_all x1, starting transfers between devices, on_device(): lax.all_to_all(part, ('x', 'zl'), split_axis=0, concat_axis=0, tiled=True)  6.3 us
    all_to_all x1, starting transfers between devices, spread_over(): return lax.all_to_all(copies, axis, split_axis=0, concat_axis=0, tiled=True)  4.94 us
    ppermute x3, waiting for transfers between devices, shifted(): return lax.ppermute(array, axis, [(i, (i + by) % n) for i in range(n)])  4.48 us
  transfers between devices with their start and end apart: 10, of which 4 were waited for; matrix products, arithmetic and copies ran while one was open for 2% of the time, Pallas kernels for 6%

profile of v4, /device:TPU:1, one launch (start us, length us, event | category | flops | bytes accessed | tf_op | source)
XLA Modules:
  0.0 157.4 jit_solution(7806167598388245338)
XLA Ops:
  7.2 0.0 all-gather.6.cloned.1.call-start
  7.2 0.7 all-gather.6.cloned.1.call-update
  7.9 1.8 %signed_rows.1 = bf16[4,4,32,512]{3,2,1,0:T(8,128)(2,1)} custom-call(s32[1,512]{1,0:T(1,128)} %bitcast.69, bf16[128,512]{1,0:T(8,128)(2,1)} %rows_ref.1), custom_call_target="tpu_custom_call" | custom-call | bytes 1048576 | tf_op jit(solution)/shard_map/signed_rows/pallas_call | solution.py:52
  9.7 9.0 %all-to-all-start = ((bf16[16,32,512]{2,1,0:T(8,128)(2,1)}), bf16[16,32,512]{2,1,0:T(8,128)(2,1)S(1)}, u32[]{:S(2)}, u32[]{:S(2)}) async-start(bf16[16,32,512]{2,1,0:T(8,128)(2,1)} %bitcast.65), calls=%async_computation | async-start | bytes 1048576 | tf_op jit(solution)/shard_map/all_to_all | solution.py:298
  18.7 0.0 all-gather.8.cloned.1.call-start
  18.8 0.2 compare_reduce_fusion
  19.1 4.5 %collective-permute-start.2 = (bf16[2,32,512]{2,1,0:T(8,128)(2,1)S(1)}, bf16[2,32,512]{2,1,0:T(8,128)(2,1)S(1)}, u32[]{:S(2)}, u32[]{:S(2)}) collective-permute-start(bf16[2,32,512]{2,1,0:T(8,128)(2,1)S(1)} %get-tuple-element.28), channel_id=1, source_target_pairs={{0,12},{4,0},{8,4},{12,8},{1,13},{5,1},{9,5},{13,9},{2,14},{6,2},{... | collective-permute-start | bytes 196616 | tf_op jit(solution)/shard_map/ppermute | solution.py:82
  23.6 2.5 %collective-permute-start.1 = (bf16[2,32,512]{2,1,0:T(8,128)(2,1)S(1)}, bf16[2,32,512]{2,1,0:T(8,128)(2,1)S(1)}, u32[]{:S(2)}, u32[]{:S(2)}) collective-permute-start(bf16[2,32,512]{2,1,0:T(8,128)(2,1)S(1)} %get-tuple-element.29), channel_id=1, source_target_pairs={{0,8},{4,12},{8,0},{12,4},{1,9},{5,13},{9,1},{13,5},{2,10},{6,14},... | collective-permute-start | bytes 196616 | tf_op jit(solution)/shard_map/ppermute | solution.py:82
  26.1 2.5 %collective-permute-start = (bf16[2,32,512]{2,1,0:T(8,128)(2,1)S(1)}, bf16[2,32,512]{2,1,0:T(8,128)(2,1)S(1)}, u32[]{:S(2)}, u32[]{:S(2)}) collective-permute-start(bf16[2,32,512]{2,1,0:T(8,128)(2,1)S(1)} %get-tuple-element.30), channel_id=1, source_target_pairs={{0,4},{4,8},{8,12},{12,0},{1,5},{5,9},{9,13},{13,1},{2,6},{6,10},{... | collective-permute-start | bytes 196616 | tf_op jit(solution)/shard_map/ppermute | solution.py:82
  28.7 4.5 %collective-permute-done = bf16[2,32,512]{2,1,0:T(8,128)(2,1)S(1)} collective-permute-done((bf16[2,32,512]{2,1,0:T(8,128)(2,1)S(1)}, bf16[2,32,512]{2,1,0:T(8,128)(2,1)S(1)}, u32[]{:S(2)}, u32[]{:S(2)}) %collective-permute-start) | collective-permute-done | bytes 65568 | tf_op jit(solution)/shard_map/ppermute | solution.py:82
  33.2 1.2 all-to-all-done
  34.4 1.5 fusion
  35.9 0.7 copy.19
  36.7 0.0 all-gather.8.cloned.1.call-update
  36.7 25.3 %all-gather = bf16[128,2048]{1,0:T(8,128)(2,1)S(1)} all-gather(bf16[32,2048]{1,0:T(8,128)(2,1)S(1)} %fusion.30), channel_id=2, replica_groups=mesh['y'=4,'zh'=4,'c'=2,'x'=4,'zl'=4] {'zh'}, dimensions={0}, use_global_device_ids=true | all-gather | bytes 655360 | tf_op jit(solution)/shard_map/all_gather | solution.py:303
  62.0 1.5 repeated.1
  63.5 4.9 %all-to-all-start.1 = ((bf16[4,128,2048]{2,1,0:T(8,128)(2,1)}), bf16[4,128,2048]{2,1,0:T(8,128)(2,1)S(1)}, u32[]{:S(2)}, u32[]{:S(2)}) async-start(bf16[4,128,2048]{2,1,0:T(8,128)(2,1)} %repeated.1), calls=%async_computation.1 | async-start | bytes 4194304 | tf_op jit(solution)/shard_map/all_to_all | solution.py:102
  68.4 26.8 %all-gather.8.cloned.1.call-done = bf16[16,2,32,512]{3,2,1,0:T(8,128)(2,1)} async-done(((bf16[4,2,32,512]{3,2,1,0:T(8,128)(2,1)}), bf16[16,2,32,512]{3,2,1,0:T(8,128)(2,1)}) %all-gather.8.cloned.1.call-update) | async-done | bytes 1048592 | tf_op jit(solution)/shard_map/all_gather | solution.py:301
  95.2 1.2 copy-done.1
  96.4 0.3 turned.1.acts_ref.refs_0_
  96.8 0.0 all-to-all-done.1
  96.8 2.8 %collective-permute-start.3 = (bf16[512,2048]{1,0:T(8,128)(2,1)S(1)}, bf16[512,2048]{1,0:T(8,128)(2,1)S(1)}, u32[]{:S(2)}, u32[]{:S(2)}) collective-permute-start(bf16[512,2048]{1,0:T(8,128)(2,1)S(1)} %bitcast.60), channel_id=1, source_target_pairs={{0,16},{16,0},{1,17},{17,1},{2,18},{18,2},{3,19},{19,3},{4,20},{20... | collective-permute-start | bytes 6291464 | tf_op jit(solution)/shard_map/ppermute | solution.py:307
  99.6 1.6 %copy-done = bf16[2048,512]{1,0:T(8,128)(2,1)S(1)} copy-done((bf16[2048,512]{1,0:T(8,128)(2,1)S(1)}, bf16[2048,512]{1,0:T(8,128)(2,1)}, u32[]{:S(2)}) %copy-start) | copy-done | bytes 2097176
  101.2 3.4 %products_own.1 = (f32[4,512,512]{2,1,0:T(8,128)S(1)}, bf16[16,2,32,512]{3,2,1,0:T(8,128)(2,1)}, bf16[4,512,512]{2,1,0:T(8,128)(2,1)}) custom-call(bf16[512,1024]{1,0:T(8,128)(2,1)S(1)} %turned.1.acts_ref.refs_0_, bf16[512,2048]{1,0:T(8,128)(2,1)S(1)} %bitcast.61, bf16[4,512,512]{2,1,0:T(8,128)(2,1)S(1)} %bitcast.62), custom_call_target="tpu_custom_call" | custom-call | flops 2147483648 | bytes 8388608 | tf_op jit(solution)/shard_map/products_own/pallas_call | solution.py:230
  104.6 3.5 %products_other.1 = (bf16[16,2,32,512]{3,2,1,0:T(8,128)(2,1)}, bf16[4,512,512]{2,1,0:T(8,128)(2,1)}) custom-call(bf16[512,1024]{1,0:T(8,128)(2,1)S(1)} %turned.1.acts_ref.refs_0_, bf16[512,2048]{1,0:T(8,128)(2,1)S(1)} %collective-permute-done.3.refs_1_, bf16[4,512,512]{2,1,0:T(8,128)(2,1)S(1)} %bitcast.63, ...), custom_call_target="tpu_custom_call", output_to_operand_aliasing={{0}: (4, {}), {1}: (5, {})} | custom-call | flops 2147483648 | bytes 8388608 | tf_op jit(solution)/shard_map/products_other/pallas_call | solution.py:244
  108.1 0.0 reduce-scatter.2.cloned.1.call-update
  108.1 6.3 %all-to-all-start.2 = ((bf16[16,2,32,512]{3,2,1,0:T(8,128)(2,1)}), bf16[16,2,32,512]{3,2,1,0:T(8,128)(2,1)S(1)}, u32[]{:S(2)}, u32[]{:S(2)}) async-start(bf16[16,2,32,512]{3,2,1,0:T(8,128)(2,1)} %get-tuple-element.24), calls=%async_computation.2 | async-start | bytes 2097152 | tf_op jit(solution)/shard_map/all_to_all | solution.py:311
  114.5 33.3 %reduce-scatter.2.cloned.1.call-done = bf16[1,512,512]{2,1,0:T(8,128)(2,1)} async-done(((bf16[4,512,512]{2,1,0:T(8,128)(2,1)}), bf16[1,512,512]{2,1,0:T(8,128)(2,1)}) %reduce-scatter.2.cloned.1.call-update) | async-done | bytes 524304 | tf_op jit(solution)/shard_map/reduce_scatter | solution.py:310
  147.8 2.0 %widen.1 = f32[512,512]{1,0:T(8,128)} custom-call(bf16[512,512]{1,0:T(8,128)(2,1)} %bitcast.70), custom_call_target="tpu_custom_call" | custom-call | flops 60000002048 | bytes 4194304 | tf_op jit(solution)/shard_map/widen/pallas_call | solution.py:268
  149.7 0.0 all-to-all-done.2
  149.7 0.2 convert_reduce_fusion
  150.0 0.9 fusion.5
  (28 shorter events, 0.3 us)
Async XLA Ops:
  7.2 11.7 %copy-start.3 = (s32[128]{0:T(128)S(1)}, s32[128]{0:T(128)}, u32[]{:S(2)}) copy-start(s32[128]{0:T(128)} %param.9) | copy-start | bytes 1540
  7.2 11.9 %copy-start.2 = (bf16[256,512]{1,0:T(8,128)(2,1)S(1)}, bf16[256,512]{1,0:T(8,128)(2,1)}, u32[]{:S(2)}) copy-start(bf16[256,512]{1,0:T(8,128)(2,1)} %param.8) | copy-start | bytes 786436
  7.2 54.8 %all-gather.6.cloned.1.call-start = ((), (), s32[]{:S(2)}) async-start(), calls=%async_computation.5 | async-start | bytes 2621440 | tf_op jit(solution)/shard_map/all_gather | solution.py:290
  9.7 24.7 %all-to-all-start = ((bf16[16,32,512]{2,1,0:T(8,128)(2,1)}), bf16[16,32,512]{2,1,0:T(8,128)(2,1)S(1)}, u32[]{:S(2)}, u32[]{:S(2)}) async-start(bf16[16,32,512]{2,1,0:T(8,128)(2,1)} %bitcast.65), calls=%async_computation | async-start | bytes 1048576 | tf_op jit(solution)/shard_map/all_to_all | solution.py:298
  18.7 76.5 %all-gather.8.cloned.1.call-start = ((), (), s32[]{:S(2)}) async-start(), calls=%async_computation.6 | async-start | bytes 1310720 | tf_op jit(solution)/shard_map/all_gather | solution.py:301
  19.1 14.1 %collective-permute-start.2 = (bf16[2,32,512]{2,1,0:T(8,128)(2,1)S(1)}, bf16[2,32,512]{2,1,0:T(8,128)(2,1)S(1)}, u32[]{:S(2)}, u32[]{:S(2)}) collective-permute-start(bf16[2,32,512]{2,1,0:T(8,128)(2,1)S(1)} %get-tuple-element.28), channel_id=1, source_target_pairs={{0,12},{4,0},{8,4},{12,8},{1,13},{5,1},{9,5},{13,9},{2,14},{6,2},{... | collective-permute-start | bytes 196616 | tf_op jit(solution)/shard_map/ppermute | solution.py:82
  23.6 9.5 %collective-permute-start.1 = (bf16[2,32,512]{2,1,0:T(8,128)(2,1)S(1)}, bf16[2,32,512]{2,1,0:T(8,128)(2,1)S(1)}, u32[]{:S(2)}, u32[]{:S(2)}) collective-permute-start(bf16[2,32,512]{2,1,0:T(8,128)(2,1)S(1)} %get-tuple-element.29), channel_id=1, source_target_pairs={{0,8},{4,12},{8,0},{12,4},{1,9},{5,13},{9,1},{13,5},{2,10},{6,14},... | collective-permute-start | bytes 196616 | tf_op jit(solution)/shard_map/ppermute | solution.py:82
  26.1 7.0 %collective-permute-start = (bf16[2,32,512]{2,1,0:T(8,128)(2,1)S(1)}, bf16[2,32,512]{2,1,0:T(8,128)(2,1)S(1)}, u32[]{:S(2)}, u32[]{:S(2)}) collective-permute-start(bf16[2,32,512]{2,1,0:T(8,128)(2,1)S(1)} %get-tuple-element.30), channel_id=1, source_target_pairs={{0,4},{4,8},{8,12},{12,0},{1,5},{5,9},{9,13},{13,1},{2,6},{6,10},{... | collective-permute-start | bytes 196616 | tf_op jit(solution)/shard_map/ppermute | solution.py:82
  63.5 33.3 %all-to-all-start.1 = ((bf16[4,128,2048]{2,1,0:T(8,128)(2,1)}), bf16[4,128,2048]{2,1,0:T(8,128)(2,1)S(1)}, u32[]{:S(2)}, u32[]{:S(2)}) async-start(bf16[4,128,2048]{2,1,0:T(8,128)(2,1)} %repeated.1), calls=%async_computation.1 | async-start | bytes 4194304 | tf_op jit(solution)/shard_map/all_to_all | solution.py:102
  68.4 79.3 %reduce-scatter.2.cloned.1.call-start = ((), (), s32[]{:S(2)}) async-start(), calls=%async_computation.4 | async-start | bytes 2621440 | tf_op jit(solution)/shard_map/reduce_scatter | solution.py:310
  95.2 1.2 copy-start.1
  96.8 7.8 %collective-permute-start.3 = (bf16[512,2048]{1,0:T(8,128)(2,1)S(1)}, bf16[512,2048]{1,0:T(8,128)(2,1)S(1)}, u32[]{:S(2)}, u32[]{:S(2)}) collective-permute-start(bf16[512,2048]{1,0:T(8,128)(2,1)S(1)} %bitcast.60), channel_id=1, source_target_pairs={{0,16},{16,0},{1,17},{17,1},{2,18},{18,2},{3,19},{19,3},{4,20},{20... | collective-permute-start | bytes 6291464 | tf_op jit(solution)/shard_map/ppermute | solution.py:307
  99.6 1.6 %copy-start = (bf16[2048,512]{1,0:T(8,128)(2,1)S(1)}, bf16[2048,512]{1,0:T(8,128)(2,1)}, u32[]{:S(2)}) copy-start(bf16[2048,512]{1,0:T(8,128)(2,1)} %all-gather.6.cloned.1.call-done) | copy-start | bytes 6291460
  108.1 41.6 %all-to-all-start.2 = ((bf16[16,2,32,512]{3,2,1,0:T(8,128)(2,1)}), bf16[16,2,32,512]{3,2,1,0:T(8,128)(2,1)S(1)}, u32[]{:S(2)}, u32[]{:S(2)}) async-start(bf16[16,2,32,512]{3,2,1,0:T(8,128)(2,1)} %get-tuple-element.24), calls=%async_computation.2 | async-start | bytes 2097152 | tf_op jit(solution)/shard_map/all_to_all | solution.py:311
Sparse Core Ops, SparseCore 0:
  10.1 43.7 all-gather.5
  56.6 38.5 all-gather.7
  108.3 39.4 reduce-scatter.1

commit v5 on v4

--- a/solution.py
+++ b/solution.py
@@ -134,7 +134,7 @@
 
 def input_part(half, rows_ref, weight_refs, part_ref, out_ref, sends):
     ff, width = weight_refs[0].shape
-    groups, quarter, _ = part_ref.shape
+    n_zl, n_x, quarter, _ = part_ref.shape
     steps = 2
     rows = rows_ref.shape[0] // steps
     out = []
@@ -147,9 +147,16 @@
                 (((1,), (1,)), ((), ())),
                 preferred_element_type=jnp.float32,
             )
-        at = pl.ds(j * (groups // steps), groups // steps)
-        part_ref[at] = total.astype(part_ref.dtype).reshape(groups // steps, quarter, ff)
-        out.append(pltpu.make_async_copy(part_ref.at[at], out_ref.at[at, half], sends.at[j]))
+        total = total.astype(part_ref.dtype)
+        each = n_x // steps
+        for group in range(each * n_zl):
+            part_ref[group % n_zl, j * each + group // n_zl] = total[
+                group * quarter : (group + 1) * quarter
+            ]
+        at = pl.ds(j * each, each)
+        out.append(
+            pltpu.make_async_copy(part_ref.at[:, at], out_ref.at[:, at, half], sends.at[j])
+        )
         out[-1].start()
     return out
 
@@ -213,18 +220,18 @@
 def products(acts, own, other, weights, quarter, scale):
     blocks, ff, width = weights.shape
     tokens, wide = own.shape
-    groups = tokens // quarter
+    n_zl = tokens // quarter // blocks
     whole = pl.BlockSpec(memory_space=pltpu.VMEM)
     hbm = pl.BlockSpec(memory_space=pltpu.HBM)
     estimate = pl.CostEstimate(
         flops=4 * ff * tokens * wide, bytes_accessed=8 * 2**20, transcendentals=0
     )
     params = pltpu.CompilerParams(vmem_limit_bytes=20 * 2**20)
-    input_shape = jax.ShapeDtypeStruct((groups, 2, quarter, ff), jnp.bfloat16)
+    input_shape = jax.ShapeDtypeStruct((n_zl, blocks, 2, quarter, ff), jnp.bfloat16)
     weight_shape = jax.ShapeDtypeStruct(weights.shape, jnp.bfloat16)
     scratch = [
         pltpu.VMEM(weights.shape, weights.dtype),
-        pltpu.VMEM((groups, quarter, ff), jnp.bfloat16),
+        pltpu.VMEM((n_zl, blocks, quarter, ff), jnp.bfloat16),
     ]
     sems = [pltpu.SemaphoreType.DMA((blocks,)), pltpu.SemaphoreType.DMA((2,))]
     first, input_part, weight_part = pl.pallas_call(
@@ -308,15 +315,15 @@
 
     parts, part = products(acts, own, other, gathered, quarter, token_scale)
     weight_grad = widen(lax.psum_scatter(parts, "x", scatter_dimension=0))
-    part = lax.all_to_all(part, ("x", "zl"), split_axis=0, concat_axis=0, tiled=True)
-    part, weight_grad = lax.optimization_barrier((part, weight_grad))
-    part = part.reshape(n_x, n_zl, 2, quarter, ff).astype(jnp.float32)
-    summed = jnp.sum(part, axis=1)
+    part = lax.all_to_all(part, "zl", split_axis=0, concat_axis=0, tiled=True)
+    part = jnp.sum(part.astype(jnp.float32), axis=0).astype(jnp.bfloat16)
+    summed = lax.all_to_all(part, "x", split_axis=0, concat_axis=0, tiled=True)
+    summed, weight_grad = lax.optimization_barrier((summed, weight_grad))
     first = jnp.where(core == 0, summed[:, 0], summed[:, 1])
     second = jnp.where(core == 0, summed[:, 1], summed[:, 0])
     summed = jnp.stack([first, second], axis=0).reshape(activations.shape)
     kept = special[None, :] | (jnp.abs(activations.astype(jnp.float32)) <= 3.0)
-    input_grad = jnp.where(kept, summed, 0.0).astype(jnp.bfloat16)
+    input_grad = jnp.where(kept, summed, 0).astype(jnp.bfloat16)
     return (input_grad, weight_grad)
 
 

time: 160 us -> 158 us (0.988); the launches traced: 157 us -> 157 us
  waiting for transfers between devices: 66.5 us -> 62.4 us
  starting transfers between devices: 32.6 us -> 35.1 us
    reduce_scatter x1, waiting for transfers between devices: 33.3 us -> 0.62 us  [on_device(): weight_grad = widen(lax.psum_scatter(parts, 'x', scatter_dimension=0))]
    all_to_all x1 -> x2, waiting for transfers between devices: 0.01 us -> 28.6 us  [the longest x1 25.7 us: on_device(): part = lax.all_to_all(part, 'zl', split_axis=0, concat_axis=0, tiled=True)]
    all_to_all x1 -> x2, starting transfers between devices: 6.3 us -> 8.85 us  [the longest x1 5.44 us: on_device(): part = lax.all_to_all(part, 'zl', split_axis=0, concat_axis=0, tiled=True)]
  transfers between devices with their start and end apart: 10 -> 11, of which waited for: 4 -> 6; matrix products, arithmetic and copies ran while one was open for 2% -> 2% of each run, Pallas kernels for 6% -> 6%
where the time goes in v5:
time: 158 us; the launch traced here: 157 us
  waiting for transfers between devices  62.4 us (39%)
  starting transfers between devices  35.1 us (22%)
  blocking collectives  25.3 us (16%)
  between operations  14.1 us (9%)
  Pallas kernels  12.8 us (8%)
  local copies, waits for them, and re-layouts  3.6 us (2%)
  other arithmetic  2.24 us (1%)
    all_gather x1, waiting for transfers between devices, on_device(): acts = lax.all_gather(acts, 'zl', axis=0)  26.8 us
    all_to_all x1, waiting for transfers between devices, on_device(): part = lax.all_to_all(part, 'zl', split_axis=0, concat_axis=0, tiled=True)  25.7 us
    all_gather x1, blocking collectives, on_device(): along = lax.all_gather(mine, 'zh', axis=0)  25.3 us
    ppermute x3, starting transfers between devices, shifted(): return lax.ppermute(array, axis, [(i, (i + by) % n) for i in range(n)])  9.45 us
    all_to_all x1, starting transfers between devices, on_device(): lax.all_to_all(spread, ('x', 'zl'), split_axis=0, concat_axis=0, tiled=True)  9.01 us
    all_to_all x1, starting transfers between devices, on_device(): part = lax.all_to_all(part, 'zl', split_axis=0, concat_axis=0, tiled=True)  5.44 us
    all_to_all x1, starting transfers between devices, spread_over(): return lax.all_to_all(copies, axis, split_axis=0, concat_axis=0, tiled=True)  4.94 us
    ppermute x3, waiting for transfers between devices, shifted(): return lax.ppermute(array, axis, [(i, (i + by) % n) for i in range(n)])  4.48 us
  transfers between devices with their start and end apart: 11, of which 6 were waited for; matrix products, arithmetic and copies ran while one was open for 2% of the time, Pallas kernels for 6%

profile of v5, /device:TPU:1, one launch (start us, length us, event | category | flops | bytes accessed | tf_op | source)
XLA Modules:
  0.0 157.0 jit_solution(11786361076461714836)
XLA Ops:
  7.2 0.0 all-gather.6.cloned.1.call-start
  7.2 0.7 all-gather.6.cloned.1.call-update
  7.9 1.8 %signed_rows.1 = bf16[4,4,32,512]{3,2,1,0:T(8,128)(2,1)} custom-call(s32[1,512]{1,0:T(1,128)} %bitcast.64, bf16[128,512]{1,0:T(8,128)(2,1)} %rows_ref.1), custom_call_target="tpu_custom_call" | custom-call | bytes 1048576 | tf_op jit(solution)/shard_map/signed_rows/pallas_call | solution.py:52
  9.7 9.0 %all-to-all-start = ((bf16[16,32,512]{2,1,0:T(8,128)(2,1)}), bf16[16,32,512]{2,1,0:T(8,128)(2,1)S(1)}, u32[]{:S(2)}, u32[]{:S(2)}) async-start(bf16[16,32,512]{2,1,0:T(8,128)(2,1)} %bitcast.60), calls=%async_computation | async-start | bytes 1048576 | tf_op jit(solution)/shard_map/all_to_all | solution.py:305
  18.7 0.0 all-gather.8.cloned.1.call-start
  18.8 0.2 compare_reduce_fusion
  19.1 4.5 %collective-permute-start.2 = (bf16[2,32,512]{2,1,0:T(8,128)(2,1)S(1)}, bf16[2,32,512]{2,1,0:T(8,128)(2,1)S(1)}, u32[]{:S(2)}, u32[]{:S(2)}) collective-permute-start(bf16[2,32,512]{2,1,0:T(8,128)(2,1)S(1)} %get-tuple-element.28), channel_id=1, source_target_pairs={{0,12},{4,0},{8,4},{12,8},{1,13},{5,1},{9,5},{13,9},{2,14},{6,2},{... | collective-permute-start | bytes 196616 | tf_op jit(solution)/shard_map/ppermute | solution.py:82
  23.6 2.5 %collective-permute-start.1 = (bf16[2,32,512]{2,1,0:T(8,128)(2,1)S(1)}, bf16[2,32,512]{2,1,0:T(8,128)(2,1)S(1)}, u32[]{:S(2)}, u32[]{:S(2)}) collective-permute-start(bf16[2,32,512]{2,1,0:T(8,128)(2,1)S(1)} %get-tuple-element.29), channel_id=1, source_target_pairs={{0,8},{4,12},{8,0},{12,4},{1,9},{5,13},{9,1},{13,5},{2,10},{6,14},... | collective-permute-start | bytes 196616 | tf_op jit(solution)/shard_map/ppermute | solution.py:82
  26.1 2.5 %collective-permute-start = (bf16[2,32,512]{2,1,0:T(8,128)(2,1)S(1)}, bf16[2,32,512]{2,1,0:T(8,128)(2,1)S(1)}, u32[]{:S(2)}, u32[]{:S(2)}) collective-permute-start(bf16[2,32,512]{2,1,0:T(8,128)(2,1)S(1)} %get-tuple-element.30), channel_id=1, source_target_pairs={{0,4},{4,8},{8,12},{12,0},{1,5},{5,9},{9,13},{13,1},{2,6},{6,10},{... | collective-permute-start | bytes 196616 | tf_op jit(solution)/shard_map/ppermute | solution.py:82
  28.7 4.5 %collective-permute-done = bf16[2,32,512]{2,1,0:T(8,128)(2,1)S(1)} collective-permute-done((bf16[2,32,512]{2,1,0:T(8,128)(2,1)S(1)}, bf16[2,32,512]{2,1,0:T(8,128)(2,1)S(1)}, u32[]{:S(2)}, u32[]{:S(2)}) %collective-permute-start) | collective-permute-done | bytes 65568 | tf_op jit(solution)/shard_map/ppermute | solution.py:82
  33.2 1.2 all-to-all-done
  34.4 1.5 fusion
  35.9 0.7 copy.19
  36.7 25.3 %all-gather = bf16[128,2048]{1,0:T(8,128)(2,1)S(1)} all-gather(bf16[32,2048]{1,0:T(8,128)(2,1)S(1)} %fusion.30), channel_id=2, replica_groups=mesh['y'=4,'zh'=4,'c'=2,'x'=4,'zl'=4] {'zh'}, dimensions={0}, use_global_device_ids=true | all-gather | bytes 655360 | tf_op jit(solution)/shard_map/all_gather | solution.py:310
  62.0 1.4 repeated.1
  63.5 4.9 %all-to-all-start.1 = ((bf16[4,128,2048]{2,1,0:T(8,128)(2,1)}), bf16[4,128,2048]{2,1,0:T(8,128)(2,1)S(1)}, u32[]{:S(2)}, u32[]{:S(2)}) async-start(bf16[4,128,2048]{2,1,0:T(8,128)(2,1)} %repeated.1), calls=%async_computation.1 | async-start | bytes 4194304 | tf_op jit(solution)/shard_map/all_to_all | solution.py:102
  68.4 26.8 %all-gather.8.cloned.1.call-done = bf16[16,2,32,512]{3,2,1,0:T(8,128)(2,1)} async-done(((bf16[4,2,32,512]{3,2,1,0:T(8,128)(2,1)}), bf16[16,2,32,512]{3,2,1,0:T(8,128)(2,1)}) %all-gather.8.cloned.1.call-update) | async-done | bytes 1048592 | tf_op jit(solution)/shard_map/all_gather | solution.py:308
  95.2 1.2 copy-done.1
  96.4 0.3 turned.1.acts_ref.refs_0_
  96.8 2.8 %collective-permute-start.3 = (bf16[512,2048]{1,0:T(8,128)(2,1)S(1)}, bf16[512,2048]{1,0:T(8,128)(2,1)S(1)}, u32[]{:S(2)}, u32[]{:S(2)}) collective-permute-start(bf16[512,2048]{1,0:T(8,128)(2,1)S(1)} %bitcast.55), channel_id=1, source_target_pairs={{0,16},{16,0},{1,17},{17,1},{2,18},{18,2},{3,19},{19,3},{4,20},{20... | collective-permute-start | bytes 6291464 | tf_op jit(solution)/shard_map/ppermute | solution.py:314
  99.6 1.6 %copy-done = bf16[2048,512]{1,0:T(8,128)(2,1)S(1)} copy-done((bf16[2048,512]{1,0:T(8,128)(2,1)S(1)}, bf16[2048,512]{1,0:T(8,128)(2,1)}, u32[]{:S(2)}) %copy-start) | copy-done | bytes 2097176
  101.2 3.6 %products_own.1 = (f32[4,512,512]{2,1,0:T(8,128)S(1)}, bf16[4,4,2,32,512]{4,3,2,1,0:T(8,128)(2,1)}, bf16[4,512,512]{2,1,0:T(8,128)(2,1)}) custom-call(bf16[512,1024]{1,0:T(8,128)(2,1)S(1)} %turned.1.acts_ref.refs_0_, bf16[512,2048]{1,0:T(8,128)(2,1)S(1)} %bitcast.56, bf16[4,512,512]{2,1,0:T(8,128)(2,1)S(1)} %bitcast.57), custom_call_target="tpu_custom_call" | custom-call | flops 2147483648 | bytes 8388608 | tf_op jit(solution)/shard_map/products_own/pallas_call | solution.py:237
  104.8 3.7 %products_other.1 = (bf16[4,4,2,32,512]{4,3,2,1,0:T(8,128)(2,1)}, bf16[4,512,512]{2,1,0:T(8,128)(2,1)}) custom-call(bf16[512,1024]{1,0:T(8,128)(2,1)S(1)} %turned.1.acts_ref.refs_0_, bf16[512,2048]{1,0:T(8,128)(2,1)S(1)} %collective-permute-done.3.refs_1_, bf16[4,512,512]{2,1,0:T(8,128)(2,1)S(1)} %bitcast.58, ...), custom_call_target="tpu_custom_call", output_to_operand_aliasing={{0}: (4, {}), {1}: (5, {})} | custom-call | flops 2147483648 | bytes 8388608 | tf_op jit(solution)/shard_map/products_other/pallas_call | solution.py:251
  108.5 0.0 reduce-scatter.2.cloned.1.call-update
  108.5 5.4 %all-to-all-start.2 = ((bf16[4,4,2,32,512]{4,3,2,1,0:T(8,128)(2,1)}), bf16[4,4,2,32,512]{4,3,2,1,0:T(8,128)(2,1)S(1)}, u32[]{:S(2)}, u32[]{:S(2)}) async-start(bf16[4,4,2,32,512]{4,3,2,1,0:T(8,128)(2,1)} %get-tuple-element.24), calls=%async_computation.2 | async-start | bytes 2097152 | tf_op jit(solution)/shard_map/all_to_all | solution.py:318
  114.0 25.7 %all-to-all-done.2 = bf16[4,4,2,32,512]{4,3,2,1,0:T(8,128)(2,1)S(1)} async-done(((bf16[4,4,2,32,512]{4,3,2,1,0:T(8,128)(2,1)}), bf16[4,4,2,32,512]{4,3,2,1,0:T(8,128)(2,1)S(1)}, u32[]{:S(2)}, u32[]{:S(2)}) %all-to-all-start.2) | async-done | bytes 1048608 | tf_op jit(solution)/shard_map/all_to_all | solution.py:318
  139.7 0.9 reduce_sum.22
  140.6 3.4 %all-to-all-start.3 = ((bf16[4,2,32,512]{3,2,1,0:T(8,128)(2,1)}), bf16[4,2,32,512]{3,2,1,0:T(8,128)(2,1)S(1)}, u32[]{:S(2)}, u32[]{:S(2)}) async-start(bf16[4,2,32,512]{3,2,1,0:T(8,128)(2,1)} %reduce_sum.22), calls=%async_computation.3 | async-start | bytes 524288 | tf_op jit(solution)/shard_map/all_to_all | solution.py:320
  144.0 0.6 reduce-scatter.2.cloned.1.call-done
  144.6 2.0 %widen.1 = f32[512,512]{1,0:T(8,128)} custom-call(bf16[512,512]{1,0:T(8,128)(2,1)} %bitcast.65), custom_call_target="tpu_custom_call" | custom-call | flops 60000002048 | bytes 4194304 | tf_op jit(solution)/shard_map/widen/pallas_call | solution.py:275
  146.6 2.9 %all-to-all-done.3 = bf16[4,2,32,512]{3,2,1,0:T(8,128)(2,1)S(1)} async-done(((bf16[4,2,32,512]{3,2,1,0:T(8,128)(2,1)}), bf16[4,2,32,512]{3,2,1,0:T(8,128)(2,1)S(1)}, u32[]{:S(2)}, u32[]{:S(2)}) %all-to-all-start.3) | async-done | bytes 262176 | tf_op jit(solution)/shard_map/all_to_all | solution.py:320
  149.6 0.9 fusion.29
  (30 shorter events, 0.3 us)
Async XLA Ops:
  7.2 11.7 %copy-start.3 = (s32[128]{0:T(128)S(1)}, s32[128]{0:T(128)}, u32[]{:S(2)}) copy-start(s32[128]{0:T(128)} %param.9) | copy-start | bytes 1540
  7.2 11.9 %copy-start.2 = (bf16[256,512]{1,0:T(8,128)(2,1)S(1)}, bf16[256,512]{1,0:T(8,128)(2,1)}, u32[]{:S(2)}) copy-start(bf16[256,512]{1,0:T(8,128)(2,1)} %param.8) | copy-start | bytes 786436
  7.2 54.8 %all-gather.6.cloned.1.call-start = ((), (), s32[]{:S(2)}) async-start(), calls=%async_computation.6 | async-start | bytes 2621440 | tf_op jit(solution)/shard_map/all_gather | solution.py:297
  9.7 24.7 %all-to-all-start = ((bf16[16,32,512]{2,1,0:T(8,128)(2,1)}), bf16[16,32,512]{2,1,0:T(8,128)(2,1)S(1)}, u32[]{:S(2)}, u32[]{:S(2)}) async-start(bf16[16,32,512]{2,1,0:T(8,128)(2,1)} %bitcast.60), calls=%async_computation | async-start | bytes 1048576 | tf_op jit(solution)/shard_map/all_to_all | solution.py:305
  18.7 76.5 %all-gather.8.cloned.1.call-start = ((), (), s32[]{:S(2)}) async-start(), calls=%async_computation.7 | async-start | bytes 1310720 | tf_op jit(solution)/shard_map/all_gather | solution.py:308
  19.1 14.1 %collective-permute-start.2 = (bf16[2,32,512]{2,1,0:T(8,128)(2,1)S(1)}, bf16[2,32,512]{2,1,0:T(8,128)(2,1)S(1)}, u32[]{:S(2)}, u32[]{:S(2)}) collective-permute-start(bf16[2,32,512]{2,1,0:T(8,128)(2,1)S(1)} %get-tuple-element.28), channel_id=1, source_target_pairs={{0,12},{4,0},{8,4},{12,8},{1,13},{5,1},{9,5},{13,9},{2,14},{6,2},{... | collective-permute-start | bytes 196616 | tf_op jit(solution)/shard_map/ppermute | solution.py:82
  23.6 9.5 %collective-permute-start.1 = (bf16[2,32,512]{2,1,0:T(8,128)(2,1)S(1)}, bf16[2,32,512]{2,1,0:T(8,128)(2,1)S(1)}, u32[]{:S(2)}, u32[]{:S(2)}) collective-permute-start(bf16[2,32,512]{2,1,0:T(8,128)(2,1)S(1)} %get-tuple-element.29), channel_id=1, source_target_pairs={{0,8},{4,12},{8,0},{12,4},{1,9},{5,13},{9,1},{13,5},{2,10},{6,14},... | collective-permute-start | bytes 196616 | tf_op jit(solution)/shard_map/ppermute | solution.py:82
  26.1 7.0 %collective-permute-start = (bf16[2,32,512]{2,1,0:T(8,128)(2,1)S(1)}, bf16[2,32,512]{2,1,0:T(8,128)(2,1)S(1)}, u32[]{:S(2)}, u32[]{:S(2)}) collective-permute-start(bf16[2,32,512]{2,1,0:T(8,128)(2,1)S(1)} %get-tuple-element.30), channel_id=1, source_target_pairs={{0,4},{4,8},{8,12},{12,0},{1,5},{5,9},{9,13},{13,1},{2,6},{6,10},{... | collective-permute-start | bytes 196616 | tf_op jit(solution)/shard_map/ppermute | solution.py:82
  63.5 33.3 %all-to-all-start.1 = ((bf16[4,128,2048]{2,1,0:T(8,128)(2,1)}), bf16[4,128,2048]{2,1,0:T(8,128)(2,1)S(1)}, u32[]{:S(2)}, u32[]{:S(2)}) async-start(bf16[4,128,2048]{2,1,0:T(8,128)(2,1)} %repeated.1), calls=%async_computation.1 | async-start | bytes 4194304 | tf_op jit(solution)/shard_map/all_to_all | solution.py:102
  68.4 76.2 %reduce-scatter.2.cloned.1.call-start = ((), (), s32[]{:S(2)}) async-start(), calls=%async_computation.5 | async-start | bytes 2621440 | tf_op jit(solution)/shard_map/reduce_scatter | solution.py:317
  95.2 1.2 copy-start.1
  96.8 8.0 %collective-permute-start.3 = (bf16[512,2048]{1,0:T(8,128)(2,1)S(1)}, bf16[512,2048]{1,0:T(8,128)(2,1)S(1)}, u32[]{:S(2)}, u32[]{:S(2)}) collective-permute-start(bf16[512,2048]{1,0:T(8,128)(2,1)S(1)} %bitcast.55), channel_id=1, source_target_pairs={{0,16},{16,0},{1,17},{17,1},{2,18},{18,2},{3,19},{19,3},{4,20},{20... | collective-permute-start | bytes 6291464 | tf_op jit(solution)/shard_map/ppermute | solution.py:314
  99.6 1.6 %copy-start = (bf16[2048,512]{1,0:T(8,128)(2,1)S(1)}, bf16[2048,512]{1,0:T(8,128)(2,1)}, u32[]{:S(2)}) copy-start(bf16[2048,512]{1,0:T(8,128)(2,1)} %all-gather.6.cloned.1.call-done) | copy-start | bytes 6291460
  108.5 31.1 %all-to-all-start.2 = ((bf16[4,4,2,32,512]{4,3,2,1,0:T(8,128)(2,1)}), bf16[4,4,2,32,512]{4,3,2,1,0:T(8,128)(2,1)S(1)}, u32[]{:S(2)}, u32[]{:S(2)}) async-start(bf16[4,4,2,32,512]{4,3,2,1,0:T(8,128)(2,1)} %get-tuple-element.24), calls=%async_computation.2 | async-start | bytes 2097152 | tf_op jit(solution)/shard_map/all_to_all | solution.py:318
  140.6 8.9 %all-to-all-start.3 = ((bf16[4,2,32,512]{3,2,1,0:T(8,128)(2,1)}), bf16[4,2,32,512]{3,2,1,0:T(8,128)(2,1)S(1)}, u32[]{:S(2)}, u32[]{:S(2)}) async-start(bf16[4,2,32,512]{3,2,1,0:T(8,128)(2,1)} %reduce_sum.22), calls=%async_computation.3 | async-start | bytes 524288 | tf_op jit(solution)/shard_map/all_to_all | solution.py:320
Sparse Core Ops, SparseCore 0:
  10.1 43.7 all-gather.5
  56.6 38.5 all-gather.7
  108.7 35.9 reduce-scatter.1

commit v6 on v5

--- a/solution.py
+++ b/solution.py
@@ -102,15 +102,23 @@
     return lax.all_to_all(copies, axis, split_axis=0, concat_axis=0, tiled=True)
 
 
-def turn_kernel(core_ref, acts_ref, out_ref, rows_ref):
+def turn_kernel(core_ref, acts_ref, out_ref, rows_ref, sems):
     n_zl, n_x, _, quarter, _ = acts_ref.shape
     tokens = n_zl * n_x * quarter
+    copies = []
     for half in range(2):
         core = jnp.bitwise_xor(core_ref[0], half)
         for i in range(n_x):
             for j in range(n_zl):
                 at = half * tokens + (i * n_zl + j) * quarter
-                rows_ref[at : at + quarter, :] = acts_ref[j, i, core]
+                copies.append(
+                    pltpu.make_async_copy(
+                        acts_ref.at[j, i, core], rows_ref.at[pl.ds(at, quarter)], sems.at[len(copies)]
+                    )
+                )
+                copies[-1].start()
+    for copy in copies:
+        copy.wait()
     out_ref[...] = rows_ref[...].T
 
 
@@ -121,11 +129,14 @@
         turn_kernel,
         in_specs=[
             pl.BlockSpec(memory_space=pltpu.SMEM),
-            pl.BlockSpec(memory_space=pltpu.VMEM),
+            pl.BlockSpec(memory_space=pltpu.HBM),
         ],
         out_specs=pl.BlockSpec(memory_space=pltpu.VMEM),
         out_shape=jax.ShapeDtypeStruct((ff, tokens), acts.dtype),
-        scratch_shapes=[pltpu.VMEM((tokens, ff), acts.dtype)],
+        scratch_shapes=[
+            pltpu.VMEM((tokens, ff), acts.dtype),
+            pltpu.SemaphoreType.DMA((acts.shape[0] * acts.shape[1] * 2,)),
+        ],
         compiler_params=pltpu.CompilerParams(vmem_limit_bytes=16 * 2**20),
         cost_estimate=pl.CostEstimate(flops=6 * 10**10, bytes_accessed=2**21, transcendentals=0),
         name="turned",

time: 158 us -> 159 us (level)
  Pallas kernels: 12.8 us -> 14.5 us
    all_to_all x1, starting transfers between devices: 5.44 us -> 3.76 us  [on_device(): part = lax.all_to_all(part, 'zl', split_axis=0, concat_axis=0, tiled=True)]
    pallas_call x1, Pallas kernels: 0.34 us -> 2.02 us  [turned(): pl.pallas_call(turn_kernel, in_specs=[pl.BlockSpec(memory_space=pltpu.SME...]
  transfers between devices with their start and end apart: 11 -> 11, of which waited for: 6 -> 6; matrix products, arithmetic and copies ran while one was open for 2% -> 2% of each run, Pallas kernels for 6% -> 7%
where the time goes in v6:
time: 159 us; the launch traced here: 158 us
  waiting for transfers between devices  62.4 us (39%)
  starting transfers between devices  34 us (21%)
  blocking collectives  25.3 us (16%)
  Pallas kernels  14.5 us (9%)
  between operations  14.1 us (9%)
  local copies, waits for them, and re-layouts  3.6 us (2%)
  other arithmetic  2.24 us (1%)
    all_gather x1, waiting for transfers between devices, on_device(): acts = lax.all_gather(acts, 'zl', axis=0)  26.8 us
    all_to_all x1, waiting for transfers between devices, on_device(): part = lax.all_to_all(part, 'zl', split_axis=0, concat_axis=0, tiled=True)  25.7 us
    all_gather x1, blocking collectives, on_device(): along = lax.all_gather(mine, 'zh', axis=0)  25.3 us
    ppermute x3, starting transfers between devices, shifted(): return lax.ppermute(array, axis, [(i, (i + by) % n) for i in range(n)])  9.45 us
    all_to_all x1, starting transfers between devices, on_device(): lax.all_to_all(spread, ('x', 'zl'), split_axis=0, concat_axis=0, tiled=True)  9.01 us
    all_to_all x1, starting transfers between devices, spread_over(): return lax.all_to_all(copies, axis, split_axis=0, concat_axis=0, tiled=True)  4.94 us
    ppermute x3, waiting for transfers between devices, shifted(): return lax.ppermute(array, axis, [(i, (i + by) % n) for i in range(n)])  4.48 us
    all_to_all x1, starting transfers between devices, on_device(): summed = lax.all_to_all(part, 'x', split_axis=0, concat_axis=0, tiled=True)  3.92 us
  transfers between devices with their start and end apart: 11, of which 6 were waited for; matrix products, arithmetic and copies ran while one was open for 2% of the time, Pallas kernels for 7%

profile of v6, /device:TPU:1, one launch (start us, length us, event | category | flops | bytes accessed | tf_op | source)
XLA Modules:
  0.0 157.6 jit_solution(8093701581940318605)
XLA Ops:
  7.2 0.0 all-gather.6.cloned.1.call-start
  7.2 0.7 all-gather.6.cloned.1.call-update
  7.9 1.8 %signed_rows.1 = bf16[4,4,32,512]{3,2,1,0:T(8,128)(2,1)} custom-call(s32[1,512]{1,0:T(1,128)} %bitcast.64, bf16[128,512]{1,0:T(8,128)(2,1)} %rows_ref.1), custom_call_target="tpu_custom_call" | custom-call | bytes 1048576 | tf_op jit(solution)/shard_map/signed_rows/pallas_call | solution.py:52
  9.7 9.0 %all-to-all-start = ((bf16[16,32,512]{2,1,0:T(8,128)(2,1)}), bf16[16,32,512]{2,1,0:T(8,128)(2,1)S(1)}, u32[]{:S(2)}, u32[]{:S(2)}) async-start(bf16[16,32,512]{2,1,0:T(8,128)(2,1)} %bitcast.60), calls=%async_computation | async-start | bytes 1048576 | tf_op jit(solution)/shard_map/all_to_all | solution.py:316
  18.7 0.0 all-gather.8.cloned.1.call-start
  18.8 0.2 compare_reduce_fusion
  19.1 4.5 %collective-permute-start.2 = (bf16[2,32,512]{2,1,0:T(8,128)(2,1)S(1)}, bf16[2,32,512]{2,1,0:T(8,128)(2,1)S(1)}, u32[]{:S(2)}, u32[]{:S(2)}) collective-permute-start(bf16[2,32,512]{2,1,0:T(8,128)(2,1)S(1)} %get-tuple-element.28), channel_id=1, source_target_pairs={{0,12},{4,0},{8,4},{12,8},{1,13},{5,1},{9,5},{13,9},{2,14},{6,2},{... | collective-permute-start | bytes 196616 | tf_op jit(solution)/shard_map/ppermute | solution.py:82
  23.6 2.5 %collective-permute-start.1 = (bf16[2,32,512]{2,1,0:T(8,128)(2,1)S(1)}, bf16[2,32,512]{2,1,0:T(8,128)(2,1)S(1)}, u32[]{:S(2)}, u32[]{:S(2)}) collective-permute-start(bf16[2,32,512]{2,1,0:T(8,128)(2,1)S(1)} %get-tuple-element.29), channel_id=1, source_target_pairs={{0,8},{4,12},{8,0},{12,4},{1,9},{5,13},{9,1},{13,5},{2,10},{6,14},... | collective-permute-start | bytes 196616 | tf_op jit(solution)/shard_map/ppermute | solution.py:82
  26.1 2.5 %collective-permute-start = (bf16[2,32,512]{2,1,0:T(8,128)(2,1)S(1)}, bf16[2,32,512]{2,1,0:T(8,128)(2,1)S(1)}, u32[]{:S(2)}, u32[]{:S(2)}) collective-permute-start(bf16[2,32,512]{2,1,0:T(8,128)(2,1)S(1)} %get-tuple-element.30), channel_id=1, source_target_pairs={{0,4},{4,8},{8,12},{12,0},{1,5},{5,9},{9,13},{13,1},{2,6},{6,10},{... | collective-permute-start | bytes 196616 | tf_op jit(solution)/shard_map/ppermute | solution.py:82
  28.7 4.5 %collective-permute-done = bf16[2,32,512]{2,1,0:T(8,128)(2,1)S(1)} collective-permute-done((bf16[2,32,512]{2,1,0:T(8,128)(2,1)S(1)}, bf16[2,32,512]{2,1,0:T(8,128)(2,1)S(1)}, u32[]{:S(2)}, u32[]{:S(2)}) %collective-permute-start) | collective-permute-done | bytes 65568 | tf_op jit(solution)/shard_map/ppermute | solution.py:82
  33.2 1.2 all-to-all-done
  34.4 1.5 fusion
  35.9 0.7 copy.19
  36.7 25.3 %all-gather = bf16[128,2048]{1,0:T(8,128)(2,1)S(1)} all-gather(bf16[32,2048]{1,0:T(8,128)(2,1)S(1)} %fusion.30), channel_id=2, replica_groups=mesh['y'=4,'zh'=4,'c'=2,'x'=4,'zl'=4] {'zh'}, dimensions={0}, use_global_device_ids=true | all-gather | bytes 655360 | tf_op jit(solution)/shard_map/all_gather | solution.py:321
  62.0 1.4 repeated.1
  63.5 4.9 %all-to-all-start.1 = ((bf16[4,128,2048]{2,1,0:T(8,128)(2,1)}), bf16[4,128,2048]{2,1,0:T(8,128)(2,1)S(1)}, u32[]{:S(2)}, u32[]{:S(2)}) async-start(bf16[4,128,2048]{2,1,0:T(8,128)(2,1)} %repeated.1), calls=%async_computation.1 | async-start | bytes 4194304 | tf_op jit(solution)/shard_map/all_to_all | solution.py:102
  68.4 26.8 %all-gather.8.cloned.1.call-done = bf16[16,2,32,512]{3,2,1,0:T(8,128)(2,1)} async-done(((bf16[4,2,32,512]{3,2,1,0:T(8,128)(2,1)}), bf16[16,2,32,512]{3,2,1,0:T(8,128)(2,1)}) %all-gather.8.cloned.1.call-update) | async-done | bytes 1048592 | tf_op jit(solution)/shard_map/all_gather | solution.py:319
  95.2 1.2 copy-done.1
  96.4 2.0 %turned.1.acts_ref.refs_0_ = bf16[512,1024]{1,0:T(8,128)(2,1)S(1)} custom-call(s32[1]{0:T(128)} %bitcast.21.core_ref, bf16[4,4,2,32,512]{4,3,2,1,0:T(8,128)(2,1)S(1)} %bitcast.59), custom_call_target="tpu_custom_call" | custom-call | flops 60000002048 | bytes 2097152 | tf_op jit(solution)/shard_map/turned/pallas_call | solution.py:128
  98.5 2.8 %collective-permute-start.3 = (bf16[512,2048]{1,0:T(8,128)(2,1)S(1)}, bf16[512,2048]{1,0:T(8,128)(2,1)S(1)}, u32[]{:S(2)}, u32[]{:S(2)}) collective-permute-start(bf16[512,2048]{1,0:T(8,128)(2,1)S(1)} %bitcast.55), channel_id=1, source_target_pairs={{0,16},{16,0},{1,17},{17,1},{2,18},{18,2},{3,19},{19,3},{4,20},{20... | collective-permute-start | bytes 6291464 | tf_op jit(solution)/shard_map/ppermute | solution.py:325
  101.3 1.6 %copy-done = bf16[2048,512]{1,0:T(8,128)(2,1)S(1)} copy-done((bf16[2048,512]{1,0:T(8,128)(2,1)S(1)}, bf16[2048,512]{1,0:T(8,128)(2,1)}, u32[]{:S(2)}) %copy-start) | copy-done | bytes 2097176
  102.9 3.6 %products_own.1 = (f32[4,512,512]{2,1,0:T(8,128)S(1)}, bf16[4,4,2,32,512]{4,3,2,1,0:T(8,128)(2,1)}, bf16[4,512,512]{2,1,0:T(8,128)(2,1)}) custom-call(bf16[512,1024]{1,0:T(8,128)(2,1)S(1)} %turned.1.acts_ref.refs_0_, bf16[512,2048]{1,0:T(8,128)(2,1)S(1)} %bitcast.56, bf16[4,512,512]{2,1,0:T(8,128)(2,1)S(1)} %bitcast.57), custom_call_target="tpu_custom_call" | custom-call | flops 2147483648 | bytes 8388608 | tf_op jit(solution)/shard_map/products_own/pallas_call | solution.py:248
  106.5 3.7 %products_other.1 = (bf16[4,4,2,32,512]{4,3,2,1,0:T(8,128)(2,1)}, bf16[4,512,512]{2,1,0:T(8,128)(2,1)}) custom-call(bf16[512,1024]{1,0:T(8,128)(2,1)S(1)} %turned.1.acts_ref.refs_0_, bf16[512,2048]{1,0:T(8,128)(2,1)S(1)} %collective-permute-done.3.refs_1_, bf16[4,512,512]{2,1,0:T(8,128)(2,1)S(1)} %bitcast.58, ...), custom_call_target="tpu_custom_call", output_to_operand_aliasing={{0}: (4, {}), {1}: (5, {})} | custom-call | flops 2147483648 | bytes 8388608 | tf_op jit(solution)/shard_map/products_other/pallas_call | solution.py:262
  110.2 0.0 reduce-scatter.2.cloned.1.call-update
  110.2 3.8 %all-to-all-start.2 = ((bf16[4,4,2,32,512]{4,3,2,1,0:T(8,128)(2,1)}), bf16[4,4,2,32,512]{4,3,2,1,0:T(8,128)(2,1)S(1)}, u32[]{:S(2)}, u32[]{:S(2)}) async-start(bf16[4,4,2,32,512]{4,3,2,1,0:T(8,128)(2,1)} %get-tuple-element.24), calls=%async_computation.2 | async-start | bytes 2097152 | tf_op jit(solution)/shard_map/all_to_all | solution.py:329
  114.0 25.7 %all-to-all-done.2 = bf16[4,4,2,32,512]{4,3,2,1,0:T(8,128)(2,1)S(1)} async-done(((bf16[4,4,2,32,512]{4,3,2,1,0:T(8,128)(2,1)}), bf16[4,4,2,32,512]{4,3,2,1,0:T(8,128)(2,1)S(1)}, u32[]{:S(2)}, u32[]{:S(2)}) %all-to-all-start.2) | async-done | bytes 1048608 | tf_op jit(solution)/shard_map/all_to_all | solution.py:329
  139.7 0.9 reduce_sum.22
  140.6 3.9 %all-to-all-start.3 = ((bf16[4,2,32,512]{3,2,1,0:T(8,128)(2,1)}), bf16[4,2,32,512]{3,2,1,0:T(8,128)(2,1)S(1)}, u32[]{:S(2)}, u32[]{:S(2)}) async-start(bf16[4,2,32,512]{3,2,1,0:T(8,128)(2,1)} %reduce_sum.22), calls=%async_computation.3 | async-start | bytes 524288 | tf_op jit(solution)/shard_map/all_to_all | solution.py:331
  144.5 1.8 %reduce-scatter.2.cloned.1.call-done = bf16[1,512,512]{2,1,0:T(8,128)(2,1)} async-done(((bf16[4,512,512]{2,1,0:T(8,128)(2,1)}), bf16[1,512,512]{2,1,0:T(8,128)(2,1)}) %reduce-scatter.2.cloned.1.call-update) | async-done | bytes 524304 | tf_op jit(solution)/shard_map/reduce_scatter | solution.py:328
  146.3 2.0 %widen.1 = f32[512,512]{1,0:T(8,128)} custom-call(bf16[512,512]{1,0:T(8,128)(2,1)} %bitcast.65), custom_call_target="tpu_custom_call" | custom-call | flops 60000002048 | bytes 4194304 | tf_op jit(solution)/shard_map/widen/pallas_call | solution.py:286
  148.3 1.8 %all-to-all-done.3 = bf16[4,2,32,512]{3,2,1,0:T(8,128)(2,1)S(1)} async-done(((bf16[4,2,32,512]{3,2,1,0:T(8,128)(2,1)}), bf16[4,2,32,512]{3,2,1,0:T(8,128)(2,1)S(1)}, u32[]{:S(2)}, u32[]{:S(2)}) %all-to-all-start.3) | async-done | bytes 262176 | tf_op jit(solution)/shard_map/all_to_all | solution.py:331
  150.2 0.9 fusion.29
  (30 shorter events, 0.3 us)
Async XLA Ops:
  7.2 11.7 %copy-start.3 = (s32[128]{0:T(128)S(1)}, s32[128]{0:T(128)}, u32[]{:S(2)}) copy-start(s32[128]{0:T(128)} %param.9) | copy-start | bytes 1540
  7.2 11.9 %copy-start.2 = (bf16[256,512]{1,0:T(8,128)(2,1)S(1)}, bf16[256,512]{1,0:T(8,128)(2,1)}, u32[]{:S(2)}) copy-start(bf16[256,512]{1,0:T(8,128)(2,1)} %param.8) | copy-start | bytes 786436
  7.2 54.8 %all-gather.6.cloned.1.call-start = ((), (), s32[]{:S(2)}) async-start(), calls=%async_computation.6 | async-start | bytes 2621440 | tf_op jit(solution)/shard_map/all_gather | solution.py:308
  9.7 24.7 %all-to-all-start = ((bf16[16,32,512]{2,1,0:T(8,128)(2,1)}), bf16[16,32,512]{2,1,0:T(8,128)(2,1)S(1)}, u32[]{:S(2)}, u32[]{:S(2)}) async-start(bf16[16,32,512]{2,1,0:T(8,128)(2,1)} %bitcast.60), calls=%async_computation | async-start | bytes 1048576 | tf_op jit(solution)/shard_map/all_to_all | solution.py:316
  18.7 76.5 %all-gather.8.cloned.1.call-start = ((), (), s32[]{:S(2)}) async-start(), calls=%async_computation.7 | async-start | bytes 1310720 | tf_op jit(solution)/shard_map/all_gather | solution.py:319
  19.1 14.1 %collective-permute-start.2 = (bf16[2,32,512]{2,1,0:T(8,128)(2,1)S(1)}, bf16[2,32,512]{2,1,0:T(8,128)(2,1)S(1)}, u32[]{:S(2)}, u32[]{:S(2)}) collective-permute-start(bf16[2,32,512]{2,1,0:T(8,128)(2,1)S(1)} %get-tuple-element.28), channel_id=1, source_target_pairs={{0,12},{4,0},{8,4},{12,8},{1,13},{5,1},{9,5},{13,9},{2,14},{6,2},{... | collective-permute-start | bytes 196616 | tf_op jit(solution)/shard_map/ppermute | solution.py:82
  23.6 9.5 %collective-permute-start.1 = (bf16[2,32,512]{2,1,0:T(8,128)(2,1)S(1)}, bf16[2,32,512]{2,1,0:T(8,128)(2,1)S(1)}, u32[]{:S(2)}, u32[]{:S(2)}) collective-permute-start(bf16[2,32,512]{2,1,0:T(8,128)(2,1)S(1)} %get-tuple-element.29), channel_id=1, source_target_pairs={{0,8},{4,12},{8,0},{12,4},{1,9},{5,13},{9,1},{13,5},{2,10},{6,14},... | collective-permute-start | bytes 196616 | tf_op jit(solution)/shard_map/ppermute | solution.py:82
  26.1 7.0 %collective-permute-start = (bf16[2,32,512]{2,1,0:T(8,128)(2,1)S(1)}, bf16[2,32,512]{2,1,0:T(8,128)(2,1)S(1)}, u32[]{:S(2)}, u32[]{:S(2)}) collective-permute-start(bf16[2,32,512]{2,1,0:T(8,128)(2,1)S(1)} %get-tuple-element.30), channel_id=1, source_target_pairs={{0,4},{4,8},{8,12},{12,0},{1,5},{5,9},{9,13},{13,1},{2,6},{6,10},{... | collective-permute-start | bytes 196616 | tf_op jit(solution)/shard_map/ppermute | solution.py:82
  63.5 35.0 %all-to-all-start.1 = ((bf16[4,128,2048]{2,1,0:T(8,128)(2,1)}), bf16[4,128,2048]{2,1,0:T(8,128)(2,1)S(1)}, u32[]{:S(2)}, u32[]{:S(2)}) async-start(bf16[4,128,2048]{2,1,0:T(8,128)(2,1)} %repeated.1), calls=%async_computation.1 | async-start | bytes 4194304 | tf_op jit(solution)/shard_map/all_to_all | solution.py:102
  68.4 77.9 %reduce-scatter.2.cloned.1.call-start = ((), (), s32[]{:S(2)}) async-start(), calls=%async_computation.5 | async-start | bytes 2621440 | tf_op jit(solution)/shard_map/reduce_scatter | solution.py:328
  95.2 1.2 copy-start.1
  98.5 8.1 %collective-permute-start.3 = (bf16[512,2048]{1,0:T(8,128)(2,1)S(1)}, bf16[512,2048]{1,0:T(8,128)(2,1)S(1)}, u32[]{:S(2)}, u32[]{:S(2)}) collective-permute-start(bf16[512,2048]{1,0:T(8,128)(2,1)S(1)} %bitcast.55), channel_id=1, source_target_pairs={{0,16},{16,0},{1,17},{17,1},{2,18},{18,2},{3,19},{19,3},{4,20},{20... | collective-permute-start | bytes 6291464 | tf_op jit(solution)/shard_map/ppermute | solution.py:325
  101.3 1.6 %copy-start = (bf16[2048,512]{1,0:T(8,128)(2,1)S(1)}, bf16[2048,512]{1,0:T(8,128)(2,1)}, u32[]{:S(2)}) copy-start(bf16[2048,512]{1,0:T(8,128)(2,1)} %all-gather.6.cloned.1.call-done) | copy-start | bytes 6291460
  110.2 29.4 %all-to-all-start.2 = ((bf16[4,4,2,32,512]{4,3,2,1,0:T(8,128)(2,1)}), bf16[4,4,2,32,512]{4,3,2,1,0:T(8,128)(2,1)S(1)}, u32[]{:S(2)}, u32[]{:S(2)}) async-start(bf16[4,4,2,32,512]{4,3,2,1,0:T(8,128)(2,1)} %get-tuple-element.24), calls=%async_computation.2 | async-start | bytes 2097152 | tf_op jit(solution)/shard_map/all_to_all | solution.py:329
  140.6 9.5 %all-to-all-start.3 = ((bf16[4,2,32,512]{3,2,1,0:T(8,128)(2,1)}), bf16[4,2,32,512]{3,2,1,0:T(8,128)(2,1)S(1)}, u32[]{:S(2)}, u32[]{:S(2)}) async-start(bf16[4,2,32,512]{3,2,1,0:T(8,128)(2,1)} %reduce_sum.22), calls=%async_computation.3 | async-start | bytes 524288 | tf_op jit(solution)/shard_map/all_to_all | solution.py:331
Sparse Core Ops, SparseCore 0:
  10.1 43.7 all-gather.5
  56.6 38.5 all-gather.7
  110.4 35.9 reduce-scatter.1
